TPU v7x, 32 devices: a whole 2x2x4 slice. The times are simulated.
32 devices in a mesh: tm: 4 (over y, x), space: 8 (over z, core).
Axes of the slice: x: 2, y: 2, z: 4, core: 2. Of those that a mesh axis runs over, the one named last changes fastest.
Arguments:
- potential: float32 [64, 64, 128, 128], P('tm', 'space'), may hold values from -6 to 6
- multiplier: float32 [4, 64, 64, 128, 128], P(None, 'tm', 'space'), may hold values from -12 to 12
- start_density: float32 [64, 128, 128], P('space'), may hold values from 0.1 to 1
- final_density: float32 [64, 128, 128], P('space'), may hold values from 0.1 to 1
Outputs:
- next_potential: float32 [64, 64, 128, 128], P('tm', 'space')
- next_multiplier: float32 [4, 64, 64, 128, 128], P(None, 'tm', 'space')
All inputs are finite; a program needn't handle non-finite values.
Results may differ from a plain program's by a relative error of at most 0.0003.
Values sent between devices are 32-bit elements; how exact they have to be, the bound alone decides.
No kernel may reach another device: no remote copies, remote signals or barrier semaphores. Data moves between devices by JAX's collectives and lax.ppermute only.
A program may use at most 256 MiB of HBM per device.

v0:
```python
import jax
import jax.numpy as jnp
from jax import lax
from jax.sharding import PartitionSpec as P

NEWTON = 10


RATE = 4.0
PROX = 0.01


def from_behind(block, axis, distance):
    devices = range(lax.axis_size(axis))
    route = [(i - distance, i) for i in devices if i - distance in devices]
    return lax.ppermute(block, axis, route)


def cosine_table(length):
    freq = jnp.arange(length, dtype=jnp.float32)[:, None]
    place = jnp.arange(length, dtype=jnp.float32)[None, :]
    weight = jnp.where(freq == 0.0, jnp.sqrt(jnp.float32(0.5)), jnp.float32(1.0))
    return (
        jnp.sqrt(jnp.float32(2.0) / length)
        * weight
        * jnp.cos(jnp.pi * freq * (place + 0.5) / length)
    )


def eigen_at(length, freq):
    return 4.0 * jnp.square(jnp.sin(jnp.pi * freq / (2.0 * length)))


def adjoint(face, axis):
    size = face.shape[axis]
    inner = lax.slice_in_dim(face, 0, size - 1, axis=axis)
    edge = jnp.zeros_like(lax.slice_in_dim(face, 0, 1, axis=axis))
    return jnp.concatenate([edge, inner], axis=axis) - jnp.concatenate([inner, edge], axis=axis)


def local_diff(field, axis):
    size = field.shape[axis]
    upper = lax.slice_in_dim(field, 1, size, axis=axis)
    lower = lax.slice_in_dim(field, 0, size - 1, axis=axis)
    edge = jnp.zeros_like(lax.slice_in_dim(field, 0, 1, axis=axis))
    return jnp.concatenate([upper - lower, edge], axis=axis)


def project(target):
    lead = target[0]
    side = target[1:]
    wsq = jnp.sum(side * side, axis=0)
    excess = lead + 0.5 * wsq
    stretch = jnp.maximum(1.0, lead + 1.0)
    for step in range(NEWTON):
        resid = stretch - (lead + 1.0) - 0.5 * wsq / (stretch * stretch)
        slope = 1.0 + wsq / (stretch * stretch * stretch)
        stretch = jnp.maximum(1.0, stretch - resid / slope)
    inside = excess <= 0.0
    new_lead = jnp.where(inside, lead, lead - (stretch - 1.0))
    new_side = jnp.where(inside[None], side, side / stretch[None])
    return jnp.concatenate([new_lead[None], new_side], axis=0)


def body(potential, multiplier, start_density, final_density):
    high = lax.Precision.HIGHEST
    steps_t, rows_x, width_y, width_z = potential.shape
    n_tm = lax.axis_size("tm")
    n_sp = lax.axis_size("space")
    total_t = steps_t * n_tm
    total_x = rows_x * n_sp
    block_y = width_y // (n_tm * n_sp)
    time_at = lax.axis_index("tm") * steps_t + jnp.arange(steps_t)
    row_at = lax.axis_index("space") * rows_x + jnp.arange(rows_x)
    not_last_t = (time_at < total_t - 1)[:, None, None, None]
    not_last_x = (row_at < total_x - 1)[None, :, None, None]
    ahead_t = from_behind(potential[:1], "tm", -1)
    ahead_x = from_behind(potential[:, :1], "space", -1)
    later = jnp.concatenate([potential[1:], ahead_t], axis=0)
    beside = jnp.concatenate([potential[:, 1:], ahead_x], axis=1)
    grad_t = jnp.where(not_last_t, later - potential, 0.0)
    grad_x = jnp.where(not_last_x, beside - potential, 0.0)
    gradient = jnp.stack([grad_t, grad_x, local_diff(potential, 2), local_diff(potential, 3)])
    projected = project(gradient + multiplier / RATE)
    next_multiplier = multiplier + RATE * (gradient - projected)
    flux = next_multiplier - RATE * projected
    rest = -(adjoint(flux[2], 2) + adjoint(flux[3], 3)) + PROX * potential
    first_step = (time_at == 0)[:, None, None, None]
    last_step = (time_at == total_t - 1)[:, None, None, None]
    rest = (
        rest
        + jnp.where(first_step, start_density[None], 0.0)
        - jnp.where(last_step, final_density[None], 0.0)
    )
    behind_t = from_behind(flux[0][-1:], "tm", 1)
    behind_x = from_behind(flux[1][:, -1:], "space", 1)
    flow_t = jnp.where(not_last_t, flux[0], 0.0)
    flow_x = jnp.where(not_last_x, flux[1], 0.0)
    div_t = jnp.concatenate([behind_t, flux[0][:-1]], axis=0) - flow_t
    div_x = jnp.concatenate([behind_x, flux[1][:, :-1]], axis=1) - flow_x
    payload = (rest - div_t - div_x)[None]
    cos_y = cosine_table(width_y)
    cos_z = cosine_table(width_z)
    payload = jnp.einsum("ctxyi,ki->ctxyk", payload, cos_z, precision=high)
    payload = jnp.einsum("ctxiz,ki->ctxkz", payload, cos_y, precision=high)
    middle = lax.all_to_all(
        lax.all_to_all(payload, "tm", split_axis=3, concat_axis=1, tiled=True),
        "space",
        split_axis=3,
        concat_axis=2,
        tiled=True,
    )
    combined = middle[0]
    cos_t = cosine_table(total_t)
    cos_x = cosine_table(total_x)
    hat = jnp.einsum("ki,ixyz->kxyz", cos_t, combined, precision=high)
    hat = jnp.einsum("ki,tiyz->tkyz", cos_x, hat, precision=high)
    freq_y = (
        (lax.axis_index("tm") * n_sp + lax.axis_index("space")) * block_y + jnp.arange(block_y)
    ).astype(jnp.float32)
    eig_t = eigen_at(total_t, jnp.arange(total_t, dtype=jnp.float32))
    eig_x = eigen_at(total_x, jnp.arange(total_x, dtype=jnp.float32))
    eig_y = eigen_at(width_y, freq_y)
    eig_z = eigen_at(width_z, jnp.arange(width_z, dtype=jnp.float32))
    denom = eig_t[:, None, None, None] + eig_x[None, :, None, None]
    denom = denom + eig_y[None, None, :, None] + eig_z[None, None, None, :]
    hat = hat / (RATE * denom + PROX)
    hat = jnp.einsum("ik,kxyz->ixyz", cos_t, hat, precision=high)
    solved = jnp.einsum("ik,tkyz->tiyz", cos_x, hat, precision=high)
    local = lax.all_to_all(
        lax.all_to_all(solved, "space", split_axis=1, concat_axis=2, tiled=True),
        "tm",
        split_axis=0,
        concat_axis=2,
        tiled=True,
    )
    local = jnp.einsum("ik,txkz->txiz", cos_y, local, precision=high)
    next_potential = jnp.einsum("ik,txyk->txyi", cos_z, local, precision=high)
    return (next_potential, next_multiplier)


def solution(mesh):
    in_specs = (
        P("tm", "space", None, None),
        P(None, "tm", "space", None, None),
        P("space", None, None),
        P("space", None, None),
    )
    out_specs = (P("tm", "space", None, None), P(None, "tm", "space", None, None))
    return jax.shard_map(body, mesh=mesh, in_specs=in_specs, out_specs=out_specs, check_vma=False)
```

profile of v0, /device:TPU:0, one launch (start us, length us, event | category | flops | bytes accessed | tf_op | source)
XLA Modules:
  0.0 1023.7 jit_solution(7801100251578177440)
XLA Ops:
  11.5 11.7 %slice_subtract_fusion = f32[16,8,128,127]{3,2,1,0:T(8,128)} fusion(f32[16,8,128,128]{3,2,1,0:T(8,128)} %param.4), kind=kLoop, calls=%fused_computation.133 | loop fusion | flops 2080768 | bytes 24969216 | tf_op jit(solution)/shard_map/sub | solution.py:46
  23.8 12.1 %slice_subtract_fusion.1 = f32[16,8,127,128]{3,2,1,0:T(8,128)} fusion(f32[16,8,128,128]{3,2,1,0:T(8,128)} %param.4), kind=kLoop, calls=%fused_computation.135 | loop fusion | flops 2080768 | bytes 24969216 | tf_op jit(solution)/shard_map/sub | solution.py:46
  36.0 12.6 %pad_bitcast_fusion = (f32[1,16,8,128,128]{4,3,2,1,0:T(8,128)}, f32[1,16,8,128,128]{4,3,2,1,0:T(8,128)}) fusion(f32[16,8,128,127]{3,2,1,0:T(8,128)} %slice_subtract_fusion, f32[16,8,127,128]{3,2,1,0:T(8,128)} %slice_subtract_fusion.1), kind=kLoop, calls=%fused_computation.132 | loop fusion | bytes 33423360 | tf_op jit(solution)/shard_map/stack | solution.py:83
  48.6 11.4 %fusion.57 = (f32[1,16,8,128,128]{4,3,2,1,0:T(8,128)}, f32[1,16,8,128,128]{4,3,2,1,0:T(8,128)}) fusion(f32[16,8,128,128]{3,2,1,0:T(8,128)} %param.4, f32[1,8,128,128]{3,2,1,0:T(8,128)S(1)} %collective-permute-done, f32[15,8,128,128]{3,2,1,0:T(8,128)S(1)} %slice-done.4, pred[16]{0:T(512)(128)(4,1)S(1)} %fusion.153, ...), kind=kLoop, calls=%fused_computation.91 | loop fusion | flops 12582912 | bytes 41943064 | tf_op jit(solution)/shard_map/stack | solution.py:83
  60.0 32.4 %multiply_add_fusion.1 = f32[4,16,8,128,128]{4,3,2,1,0:T(8,128)} fusion(f32[4,16,8,128,128]{4,3,2,1,0:T(8,128)} %param.5, f32[1,16,8,128,128]{4,3,2,1,0:T(8,128)} %get-tuple-element.14, f32[1,16,8,128,128]{4,3,2,1,0:T(8,128)} %get-tuple-element.15, f32[1,16,8,128,128]{4,3,2,1,0:T(8,128)} %get-tuple-element.11, f32[1,16,8,128,128]{4,3,2,1,0:T(8,128)} %get-tuple-element.10), kind=kLoop, calls=%fused_computation.5 | loop fusion | flops 41943040 | bytes 100663296 | tf_op jit(solution)/shard_map/add | solution.py:84
  92.5 15.6 %multiply_reduce_fusion = f32[16,8,128,128]{3,2,1,0:T(8,128)} fusion(f32[4,16,8,128,128]{4,3,2,1,0:T(8,128)} %multiply_add_fusion.1), kind=kLoop, calls=%fused_computation.6 | loop fusion | flops 10485760 | bytes 33554432 | tf_op jit(solution)/shard_map/reduce_sum | solution.py:52
  108.1 48.5 %subtract_select_fusion = (f32[1,16,8,128,128]{4,3,2,1,0:T(8,128)}, pred[1,16,8,128,128]{4,3,2,1,0:T(8,128)(4,1)S(1)}, f32[1,16,8,128,128]{4,3,2,1,0:T(8,128)}) fusion(f32[4,16,8,128,128]{4,3,2,1,0:T(8,128)} %multiply_add_fusion.1, f32[16,8,128,128]{3,2,1,0:T(8,128)} %multiply_reduce_fusion), kind=kLoop, calls=%fused_computation.7 | loop fusion | flops 226492416 | bytes 35651584 | tf_op jit(solution)/shard_map/jit(_where)/select_n | solution.py:60
  156.7 13.0 %divide_select_fusion = f32[3,16,8,128,128]{4,3,2,1,0:T(8,128)} fusion(f32[4,16,8,128,128]{4,3,2,1,0:T(8,128)S(1)} %bitcast.160, f32[16,8,128,128]{3,2,1,0:T(8,128)} %bitcast.169, pred[16,8,128,128]{3,2,1,0:T(8,128)(4,1)S(1)} %bitcast.172), kind=kLoop, calls=%fused_computation | loop fusion | flops 12582912 | bytes 60817408 | tf_op jit(solution)/shard_map/jit(_where)/select_n | solution.py:61
  169.7 53.1 %multiply_subtract_fusion = (f32[4,16,8,128,128]{4,3,2,1,0:T(8,128)}, f32[4,16,8,128,128]{4,3,2,1,0:T(8,128)}) fusion(f32[3,16,8,128,128]{4,3,2,1,0:T(8,128)} %divide_select_fusion, f32[1,16,8,128,128]{4,3,2,1,0:T(8,128)} %get-tuple-element.4, f32[4,16,8,128,128]{4,3,2,1,0:T(8,128)} %param.5, f32[1,16,8,128,128]{4,3,2,1,0:T(8,128)} %get-tuple-element.14, ...), kind=kLoop, calls=%fused_computation.3 | loop fusion | flops 75497472 | bytes 167772160 | tf_op jit(solution)/shard_map/sub | solution.py:86
  222.9 17.7 %slice_bitcast_fusion.3 = (f32[16,8,128,128]{3,2,1,0:T(8,128)}, f32[16,8,128,128]{3,2,1,0:T(8,128)}, f32[16,8,128,128]{3,2,1,0:T(8,128)}) fusion(f32[4,16,8,128,128]{4,3,2,1,0:T(8,128)} %get-tuple-element.2), kind=kLoop, calls=%fused_computation.88 | loop fusion | bytes 50331648 | tf_op jit(solution)/shard_map/squeeze | solution.py:87
  245.0 7.0 slice.107
  253.2 5.8 collective-permute-start.2
  259.0 7.3 slice_bitcast_fusion.4
  271.5 28.1 %fusion.54 = f32[16,8,128,128]{3,2,1,0:T(8,128)} fusion(f32[4,16,8,128,128]{4,3,2,1,0:T(8,128)} %get-tuple-element.2, f32[15,8,128,128]{3,2,1,0:T(8,128)} %slice_bitcast_fusion.4, f32[1,8,128,128]{3,2,1,0:T(8,128)} %copy-done, f32[16,7,128,128]{3,2,1,0:T(8,128)} %slice.107, f32[16,1,128,128]{3,2,1,0:T(8,128)S(1)} %collective-permute-done.3, ...), kind=kOutput, calls=%fused_computation.86 | convolution fusion | flops 3263217664 | bytes 84808192 | tf_op jit(solution)/shard_map/ctxyi,ki->ctxyk/dot_general | solution.py:104
  299.6 10.8 %convolution_bitcast_fusion = f32[1,16,8,128,128]{4,3,2,1,0:T(8,128)S(1)} fusion(f32[16,8,128,128]{3,2,1,0:T(8,128)} %fusion.54, f32[128]{0:T(128)S(1)} %get-tuple-element.17, f32[128]{0:T(128)S(1)} %iota_multiply_fusion, f32[128]{0:T(128)S(1)} %get-tuple-element.16), kind=kOutput, calls=%fused_computation.149 | convolution fusion | flops 3221274624 | bytes 16778752 | tf_op jit(solution)/shard_map/ctxiz,ki->ctxkz/dot_general | solution.py:105
  310.4 4.9 copy.20
  315.3 99.2 %all_to_all.69 = f32[1,16,8,128,128]{4,2,1,0,3:T(8,128)S(1)} all-to-all(f32[1,16,8,128,128]{4,2,1,0,3:T(8,128)S(1)} %copy.20), channel_id=1, replica_groups=mesh['tm'=4,'space'=8] {'tm'}, dimensions={3} | all-to-all | bytes 16777216 | tf_op jit(solution)/shard_map/all_to_all | solution.py:107
  414.5 4.9 copy.21
  420.8 8.3 copy.23
  429.0 5.2 all-to-all-start.1
  434.6 183.3 %all-to-all-done.1 = f32[1,64,8,32,128]{4,2,1,0,3:T(8,128)} async-done(((f32[1,64,8,32,128]{4,2,1,0,3:T(8,128)}), f32[1,64,8,32,128]{4,2,1,0,3:T(8,128)}, u32[]{:S(2)}, u32[]{:S(2)}) %all-to-all-start.1) | async-done | bytes 8388640 | tf_op jit(solution)/shard_map/all_to_all | solution.py:106
  617.9 4.5 copy.24
  623.6 16.0 %fusion.75 = f32[64,64,4,128]{3,0,2,1:T(8,128)S(1)} fusion(f32[64,64,4,128]{3,1,2,0:T(8,128)S(1)} %bitcast.162, f32[64]{0:T(128)S(1)} %get-tuple-element.19, f32[64]{0:T(128)S(1)} %iota_multiply_fusion.1, f32[64]{0:T(128)S(1)} %get-tuple-element.18), kind=kOutput, calls=%fused_computation.114 | convolution fusion | flops 1610625024 | bytes 16777984 | tf_op jit(solution)/shard_map/ki,ixyz->kxyz/dot_general | solution.py:116
  639.6 16.5 %bitcast_divide_fusion = f32[64,64,4,128]{3,1,2,0:T(8,128)S(1)} fusion(f32[128]{0:T(128)S(1)} %multiply_multiply_fusion.10, f32[64,64,4]{1,2,0:T(4,128)S(1)} %broadcast_add_fusion, f32[64,64,4,128]{3,0,2,1:T(8,128)S(1)} %fusion.75, f32[64]{0:T(128)S(1)} %get-tuple-element.19, f32[64]{0:T(128)S(1)} %iota_multiply_fusion.1, f32[64]{0:T(128)S(1)} %get-tuple-element.18), kind=kOutput, calls=%fused_computation.103 | convolution fusion | flops 1619013632 | bytes 16844032 | tf_op jit(solution)/shard_map/ki,tiyz->tkyz/dot_general | solution.py:117
  656.1 15.8 %fusion.71 = f32[64,64,4,128]{3,0,2,1:T(8,128)S(1)} fusion(f32[64,64,4,128]{3,1,2,0:T(8,128)S(1)} %bitcast_divide_fusion, f32[64]{0:T(128)S(1)} %get-tuple-element.19, f32[64]{0:T(128)S(1)} %iota_multiply_fusion.1, f32[64]{0:T(128)S(1)} %get-tuple-element.18), kind=kOutput, calls=%fused_computation.110 | convolution fusion | flops 1610625024 | bytes 16777984 | tf_op jit(solution)/shard_map/ik,kxyz->ixyz/dot_general | solution.py:128
  672.0 17.9 %fusion.103 = f32[64,64,4,128]{3,1,2,0:T(8,128)} fusion(f32[64,64,4,128]{3,0,2,1:T(8,128)S(1)} %fusion.71, f32[64]{0:T(128)S(1)} %get-tuple-element.19, f32[64]{0:T(128)S(1)} %iota_multiply_fusion.1, f32[64]{0:T(128)S(1)} %get-tuple-element.18), kind=kOutput, calls=%fused_computation.148 | convolution fusion | flops 1610625024 | bytes 16777984 | tf_op jit(solution)/shard_map/ik,tkyz->tiyz/dot_general | solution.py:129
  689.9 12.1 %copy.30 = f32[64,64,4,128]{3,2,0,1:T(4,128)} copy(f32[64,64,4,128]{3,1,2,0:T(8,128)} %fusion.103) | data formatting | bytes 16777216 | tf_op jit(solution)/shard_map/ik,tkyz->tiyz/transpose | solution.py:129
  701.9 187.9 %all_to_all.70 = f32[64,64,4,128]{3,2,0,1:T(4,128)S(1)} all-to-all(f32[64,64,4,128]{3,2,0,1:T(4,128)} %copy.30), channel_id=1, replica_groups=mesh['tm'=4,'space'=8] {'space'}, dimensions={1} | all-to-all | bytes 16777216 | tf_op jit(solution)/shard_map/all_to_all | solution.py:131
  889.9 4.9 copy.54
  895.8 95.4 %all_to_all.71 = f32[64,8,32,128]{3,1,2,0:T(8,128)S(1)} all-to-all(f32[64,8,32,128]{3,1,2,0:T(8,128)S(1)} %bitcast.167), channel_id=1, replica_groups=mesh['tm'=4,'space'=8] {'tm'}, dimensions={0} | all-to-all | bytes 16777216 | tf_op jit(solution)/shard_map/all_to_all | solution.py:130
  992.7 14.2 %fusion.109 = f32[16,8,128,128]{3,2,1,0:T(8,128)S(1)} fusion(f32[16,8,128,128]{3,2,1,0:T(8,128)S(1)} %bitcast.161, f32[128]{0:T(128)S(1)} %get-tuple-element.17, f32[128]{0:T(128)S(1)} %iota_multiply_fusion, f32[128]{0:T(128)S(1)} %get-tuple-element.16), kind=kOutput, calls=%fused_computation.152 | convolution fusion | flops 3221274624 | bytes 16778752 | tf_op jit(solution)/shard_map/ik,txkz->txiz/dot_general | solution.py:137
  1006.9 16.4 %fusion.65 = f32[16,8,128,128]{3,2,1,0:T(8,128)} fusion(f32[16,8,128,128]{3,2,1,0:T(8,128)S(1)} %fusion.109, f32[128]{0:T(128)S(1)} %get-tuple-element.17, f32[128]{0:T(128)S(1)} %iota_multiply_fusion, f32[128]{0:T(128)S(1)} %get-tuple-element.16), kind=kOutput, calls=%fused_computation.101 | convolution fusion | flops 3221274624 | bytes 16778752 | tf_op jit(solution)/shard_map/ik,txyk->txyi/dot_general | solution.py:138
  (65 shorter events, 27.7 us)
Async XLA Ops:
  1.9 4.0 slice-start
  2.0 46.7 %collective-permute-start.1 = (f32[16,1,128,128]{3,2,1,0:T(8,128)S(1)}, f32[16,1,128,128]{3,2,1,0:T(8,128)S(1)}, u32[]{:S(2)}, u32[]{:S(2)}) collective-permute-start(f32[16,1,128,128]{3,2,1,0:T(8,128)S(1)} %slice.77), channel_id=1, source_target_pairs={{1,0},{2,1},{3,2},{4,3},{5,4},{6,5},{7,6},{9,8},{10,9},{11,10},{12... | collective-permute-start | bytes 3145736 | tf_op jit(solution)/shard_map/ppermute | solution.py:16
  4.6 44.0 %collective-permute-start = (f32[1,8,128,128]{3,2,1,0:T(8,128)S(1)}, f32[1,8,128,128]{3,2,1,0:T(8,128)S(1)}, u32[]{:S(2)}, u32[]{:S(2)}) collective-permute-start(f32[1,8,128,128]{3,2,1,0:T(8,128)S(1)} %slice.75), channel_id=1, source_target_pairs={{8,0},{16,8},{24,16},{9,1},{17,9},{25,17},{10,2},{18,10},{26,18},{... | collective-permute-start | bytes 1572872 | tf_op jit(solution)/shard_map/ppermute | solution.py:16
  5.9 2.2 slice-start.1
  36.0 12.7 %slice-start.4 = ((f32[16,8,128,128]{3,2,1,0:T(8,128)}), f32[15,8,128,128]{3,2,1,0:T(8,128)S(1)}, s32[]{:S(2)}) async-start(f32[16,8,128,128]{3,2,1,0:T(8,128)} %param.4), calls=%async_computation.8 | async-start | bytes 15728640 | tf_op jit(solution)/shard_map/slice | solution.py:79
  92.4 64.2 %slice-start.5 = ((s8[33554432]{0:T(1024)(128)(4,1)}), s8[4194304]{0:T(1024)(128)(4,1)S(1)}, s32[]{:S(2)}) async-start(s8[33554432]{0:T(1024)(128)(4,1)} %bitcast.159), calls=%async_computation.9 | async-start | bytes 8388608
  92.4 64.2 %slice-start.6 = ((s8[33554432]{0:T(1024)(128)(4,1)}), s8[4194304]{0:T(1024)(128)(4,1)S(1)}, s32[]{:S(2)}) async-start(s8[33554432]{0:T(1024)(128)(4,1)} %bitcast.159), calls=%async_computation.10 | async-start | bytes 8388608
  92.4 64.2 %slice-start.7 = ((s8[33554432]{0:T(1024)(128)(4,1)}), s8[4194304]{0:T(1024)(128)(4,1)S(1)}, s32[]{:S(2)}) async-start(s8[33554432]{0:T(1024)(128)(4,1)} %bitcast.159), calls=%async_computation.11 | async-start | bytes 8388608
  92.5 64.2 %slice-start.8 = ((s8[33554432]{0:T(1024)(128)(4,1)}), s8[4194304]{0:T(1024)(128)(4,1)S(1)}, s32[]{:S(2)}) async-start(s8[33554432]{0:T(1024)(128)(4,1)} %bitcast.159), calls=%async_computation.12 | async-start | bytes 8388608
  108.1 48.6 %slice-start.9 = ((s8[33554432]{0:T(1024)(128)(4,1)}), s8[4194304]{0:T(1024)(128)(4,1)S(1)}, s32[]{:S(2)}) async-start(s8[33554432]{0:T(1024)(128)(4,1)} %bitcast.159), calls=%async_computation.13 | async-start | bytes 8388608
  108.1 48.6 %slice-start.10 = ((s8[33554432]{0:T(1024)(128)(4,1)}), s8[4194304]{0:T(1024)(128)(4,1)S(1)}, s32[]{:S(2)}) async-start(s8[33554432]{0:T(1024)(128)(4,1)} %bitcast.159), calls=%async_computation.14 | async-start | bytes 8388608
  108.1 48.6 %slice-start.11 = ((s8[33554432]{0:T(1024)(128)(4,1)}), s8[4194304]{0:T(1024)(128)(4,1)S(1)}, s32[]{:S(2)}) async-start(s8[33554432]{0:T(1024)(128)(4,1)} %bitcast.159), calls=%async_computation.15 | async-start | bytes 8388608
  108.1 48.6 %slice-start.12 = ((s8[33554432]{0:T(1024)(128)(4,1)}), s8[4194304]{0:T(1024)(128)(4,1)S(1)}, s32[]{:S(2)}) async-start(s8[33554432]{0:T(1024)(128)(4,1)} %bitcast.159), calls=%async_computation.16 | async-start | bytes 8388608
  241.9 28.8 %collective-permute-start.3 = (f32[16,1,128,128]{3,2,1,0:T(8,128)S(1)}, f32[16,1,128,128]{3,2,1,0:T(8,128)S(1)}, u32[]{:S(2)}, u32[]{:S(2)}) collective-permute-start(f32[16,1,128,128]{3,2,1,0:T(8,128)S(1)} %slice.106), channel_id=1, source_target_pairs={{0,1},{1,2},{2,3},{3,4},{4,5},{5,6},{6,7},{8,9},{9,10},{10,11},{11... | collective-permute-start | bytes 3145736 | tf_op jit(solution)/shard_map/ppermute | solution.py:16
  252.0 19.5 %slice-start.2 = ((s8[8388608]{0:T(1024)(128)(4,1)}), s8[4194304]{0:T(1024)(128)(4,1)S(1)}, s32[]{:S(2)}) async-start(s8[8388608]{0:T(1024)(128)(4,1)} %bitcast.157), calls=%async_computation.6 | async-start | bytes 8388608
  252.0 19.5 %copy-start.1 = (pred[16]{0:T(512)(128)(4,1)S(1)}, pred[16]{0:T(512)(128)(4,1)}, u32[]{:S(2)}) copy-start(pred[16]{0:T(512)(128)(4,1)} %get-tuple-element.12) | copy-start | bytes 52
  252.0 19.5 %copy-start.2 = (pred[16]{0:T(512)(128)(4,1)S(1)}, pred[16]{0:T(512)(128)(4,1)}, u32[]{:S(2)}) copy-start(pred[16]{0:T(512)(128)(4,1)} %get-tuple-element.13) | copy-start | bytes 52
  252.0 19.5 %copy-start.3 = (pred[128]{0:T(512)(128)(4,1)S(1)}, pred[128]{0:T(512)(128)(4,1)}, u32[]{:S(2)}) copy-start(pred[128]{0:T(512)(128)(4,1)} %constant.16.clone.1) | copy-start | bytes 388
  253.2 18.3 %slice-start.3 = ((s8[8388608]{0:T(1024)(128)(4,1)}), s8[4194304]{0:T(1024)(128)(4,1)S(1)}, s32[]{:S(2)}) async-start(s8[8388608]{0:T(1024)(128)(4,1)} %bitcast.157), calls=%async_computation.7 | async-start | bytes 8388608
  253.2 17.4 %collective-permute-start.2 = (f32[1,8,128,128]{3,2,1,0:T(8,128)S(1)}, f32[1,8,128,128]{3,2,1,0:T(8,128)S(1)}, u32[]{:S(2)}, u32[]{:S(2)}) collective-permute-start(f32[1,8,128,128]{3,2,1,0:T(8,128)S(1)} %slice_bitcast_fusion.5), channel_id=1, source_target_pairs={{0,8},{8,16},{16,24},{1,9},{9,17},{17,25},{2,10},{10,18},{18,26},{... | collective-permute-start | bytes 1572872 | tf_op jit(solution)/shard_map/ppermute | solution.py:16
  270.7 0.8 copy-start
  429.0 188.9 %all-to-all-start.1 = ((f32[1,64,8,32,128]{4,2,1,0,3:T(8,128)}), f32[1,64,8,32,128]{4,2,1,0,3:T(8,128)}, u32[]{:S(2)}, u32[]{:S(2)}) async-start(f32[1,64,8,32,128]{4,2,1,0,3:T(8,128)} %copy.23), calls=%async_computation.1 | async-start | bytes 16777216 | tf_op jit(solution)/shard_map/all_to_all | solution.py:106
where the time goes:
time: 1030 us; the launch traced here: 1020 us
  blocking collectives  383 us (37%)
  other arithmetic  199 us (19%)
  waiting for transfers between devices  188 us (18%)
  matrix products  136 us (13%)
  local copies, waits for them, and re-layouts  101 us (10%)
  starting transfers between devices  16.9 us (2%)
    all_to_all x1, blocking collectives, body(): lax.all_to_all(solved, 'space', split_axis=1, concat_axis=2, tiled=True)  188 us
    all_to_all x1, waiting for transfers between devices, body(): lax.all_to_all(lax.all_to_all(payload, 'tm', split_axis=3, concat_axis=1,...  183 us
    all_to_all x1, blocking collectives, body(): lax.all_to_all(payload, 'tm', split_axis=3, concat_axis=1, tiled=True)  99.2 us
    all_to_all x1, blocking collectives, body(): lax.all_to_all(lax.all_to_all(solved, 'space', split_axis=1, concat_axis=...  95.4 us
    sub x1, other arithmetic, body(): flux = next_multiplier - RATE * projected  53.1 us
    select_n x1, other arithmetic, project(): new_lead = jnp.where(inside, lead, lead - (stretch - 1.0))  48.5 us
    add x1, other arithmetic, body(): projected = project(gradient + multiplier / RATE)  32.4 us
    dot_general x1, matrix products, body(): payload = jnp.einsum('ctxyi,ki->ctxyk', payload, cos_z, precision=high)  28.1 us
  transfers between devices with their start and end apart: 5, of which 2 were waited for; matrix products, arithmetic and copies ran while one was open for 6% of the time, Pallas kernels for 0%

commit v1 on v0

v1 whole, which is shorter than its diff:
```python
import math

import jax
import jax.numpy as jnp
import numpy as np
from jax import lax
from jax.experimental import pallas as pl
from jax.experimental.pallas import tpu as pltpu
from jax.sharding import PartitionSpec as P

NEWTON = 10
RATE = 4.0
PROX = 0.01
LANES = 128
GROUP = 8
BATCH = 8
PIECES = 2
VMEM_LIMIT = 56 * 1024 * 1024


def cosine_table(length):
    freq = np.arange(length, dtype=np.float64)[:, None]
    place = np.arange(length, dtype=np.float64)[None, :]
    weight = np.where(freq == 0.0, np.sqrt(0.5), 1.0)
    return np.sqrt(2.0 / length) * weight * np.cos(np.pi * freq * (place + 0.5) / length)


def eigen(length):
    return 4.0 * np.square(np.sin(np.pi * np.arange(length) / (2.0 * length)))


def dct(xs, scale=1.0):
    n = len(xs)
    if n == 1:
        return [xs[0] * scale]
    h = n // 2
    even = dct([xs[i] + xs[n - 1 - i] for i in range(h)], scale * math.sqrt(0.5))
    diff = [xs[i] - xs[n - 1 - i] for i in range(h)]
    out = []
    for k in range(h):
        total = None
        for i in range(h):
            c = scale * math.sqrt(2.0 / n) * math.cos(math.pi * (2 * k + 1) * (i + 0.5) / n)
            term = diff[i] * c
            total = term if total is None else total + term
        out += [even[k], total]
    return out


def halves(x):
    top = x.astype(jnp.bfloat16)
    return top, (x - top.astype(jnp.float32)).astype(jnp.bfloat16)


def right_mm(x, table):
    top, low = halves(x)
    return jnp.dot(jnp.concatenate([top, low, top], axis=1), table, preferred_element_type=jnp.float32)


def left_mm(table, x):
    top, low = halves(x)
    return jnp.dot(table, jnp.concatenate([top, low, top], axis=0), preferred_element_type=jnp.float32)


def plane_mm(planes, left, right):
    n = len(planes)
    size, lanes = planes[0].shape
    half = right_mm(jnp.concatenate(planes, axis=0), right)
    half = jnp.concatenate([half[i * size : (i + 1) * size] for i in range(n)], axis=1)
    full = left_mm(left, half)
    return [full[:, i * lanes : (i + 1) * lanes] for i in range(n)]


def refined(d):
    r = pl.reciprocal(d, approx=True)
    return r * (2.0 - d * r)


def pointwise_kernel(n_in, first_row, lead, count, rows, steps, n_tm, *refs):
    flags, pot, nxt, ht, mult, start, final, cz, cy = refs[:9]
    at_end = first_row + count == rows
    fx_in = None if lead else refs[9]
    hx = refs[9 + (not lead)] if at_end else None
    nm, fx_out = refs[n_in : n_in + 2]
    pay = refs[n_in + 2 : n_in + 2 + n_tm]
    rhs, fx, ft, fyb = refs[n_in + 2 + n_tm :]
    i = pl.program_id(0)
    width = pot.shape[2]
    height = width // PIECES
    block = width // n_tm
    batch = min(BATCH, steps // 2)
    has_t, has_x, first_t, last_t = flags[0, 0], flags[0, 1], flags[0, 2], flags[0, 3]

    @pl.when(i == 0)
    def _():
        fx[...] = jnp.zeros_like(fx) if lead else fx_in[...]
        fyb[...] = jnp.zeros_like(fyb)

    def transform(t, n):
        for k, full in enumerate(plane_mm([rhs[t + k] for k in range(n)], cy[...], cz[...])):
            for d in range(n_tm):
                pay[d][t + k, 0] = full[d * block : (d + 1) * block]

    def plane(t, is_last):
        end_row = i == lead + rows - 1 - first_row
        gate_x = jnp.where(end_row, has_x, 1.0)
        lane = lax.broadcasted_iota(jnp.int32, (height, LANES), 1)
        row = lax.broadcasted_iota(jnp.int32, (height, LANES), 0)
        for part in range(PIECES):
            at = pl.ds(part * height, height)
            p = pot[t, 0, at, :]
            if is_last:
                gt = (ht[0, 0, at, :] - p) * has_t
            else:
                gt = pot[t + 1, 0, at, :] - p
            beside = nxt[t, 0, at, :]
            if at_end:
                beside = jnp.where(end_row, hx[t, 0, at, :], beside)
                gx = (beside - p) * gate_x
            else:
                gx = beside - p
            if part < PIECES - 1:
                gy = pot[t, 0, pl.ds(part * height + 1, height), :] - p
            else:
                gy = jnp.where(row == height - 1, 0.0, pltpu.roll(p, height - 1, 0) - p)
            gz = jnp.where(lane == LANES - 1, 0.0, pltpu.roll(p, LANES - 1, 1) - p)
            a = gt + mult[0, t, 0, at, :] * (1.0 / RATE)
            b1 = gx + mult[1, t, 0, at, :] * (1.0 / RATE)
            b2 = gy + mult[2, t, 0, at, :] * (1.0 / RATE)
            b3 = gz + mult[3, t, 0, at, :] * (1.0 / RATE)
            w = b1 * b1 + b2 * b2 + b3 * b3
            c = a + 1.0
            w15 = 1.5 * w
            s = jnp.maximum(1.0, c)
            for step in range(NEWTON):
                sq = s * s
                d = s * sq + w
                inv = refined(d) if step == NEWTON - 1 else pl.reciprocal(d, approx=True)
                s = jnp.maximum(1.0, s * (c * sq + w15) * inv)
            inside = a + 0.5 * w <= 0.0
            shift = jnp.where(inside, 0.0, s - 1.0)
            k = shift * refined(s)
            k4 = k * RATE
            k8 = k4 * 2.0 - RATE
            nm[0, t, 0, at, :] = shift * RATE
            nm[1, t, 0, at, :] = b1 * k4
            nm[2, t, 0, at, :] = b2 * k4
            nm[3, t, 0, at, :] = b3 * k4
            f0 = shift * (2.0 * RATE) - a * RATE
            f1 = b1 * k8
            f2 = b2 * k8
            f3 = b3 * k8
            if part == PIECES - 1:
                f2 = jnp.where(row == height - 1, 0.0, f2)
            f3 = jnp.where(lane == LANES - 1, 0.0, f3)
            if at_end:
                f1 = f1 * gate_x
            fyb[pl.ds(GROUP + part * height, height), :] = f2
            total = PROX * p + (f1 - fx[t, at, :]) + (f3 - pltpu.roll(f3, 1, 1))
            total = total + (f2 - fyb[pl.ds(GROUP - 1 + part * height, height), :])
            total = total - ft[at, :]
            if is_last:
                total = total - final[0, at, :] * last_t
                rhs[steps, at, :] = f0
            else:
                total = total + f0
                ft[at, :] = f0
            fx[t, at, :] = f1
            rhs[t, at, :] = total

    ft[...] = start[0] * (-first_t)
    for k in range(batch):
        plane(k, False)

    def step_of(b, carry):
        transform((b - 1) * batch, batch)
        for k in range(batch):
            plane(b * batch + k, False)
        return carry

    lax.fori_loop(1, steps // batch - 1, step_of, 0)
    transform(steps - 2 * batch, batch)
    for k in range(batch):
        plane(steps - batch + k, k == batch - 1)
    transform(steps - batch, batch)
    transform(steps, 1)

    @pl.when(i == lead + count - 1)
    def _():
        fx_out[...] = fx[...]


def thirds(table):
    table = np.asarray(table, np.float32)
    top = table.astype(jnp.bfloat16)
    low = (table - top.astype(np.float32)).astype(jnp.bfloat16)
    return jnp.asarray(np.stack([top, top, low]))


def cost(cells, picoseconds):
    return pl.CostEstimate(flops=int(cells * picoseconds * 1150), bytes_accessed=0, transcendentals=0)


def params():
    return pltpu.CompilerParams(vmem_limit_bytes=VMEM_LIMIT)


def pointwise(first_row, lead, count, n_tm, operands, tables, fx_in, nm):
    potential, multiplier = operands[1], operands[2]
    steps, rows, width, _ = potential.shape
    flags, potential, multiplier, start, final, ahead_t, ahead_x = operands
    here = lambda i: jnp.minimum(first_row - lead + i, rows - 1)
    slot = lambda i: jnp.maximum(i - lead, 0)
    plane = (width, LANES)
    block = width // n_tm
    in_specs = [
        pl.BlockSpec(memory_space=pltpu.SMEM),
        pl.BlockSpec((steps, 1) + plane, lambda i: (0, here(i), 0, 0)),
        pl.BlockSpec((steps, 1) + plane, lambda i: (0, here(i + 1), 0, 0)),
        pl.BlockSpec((1, 1) + plane, lambda i: (0, here(i), 0, 0)),
        pl.BlockSpec((4, steps, 1) + plane, lambda i: (0, 0, here(i), 0, 0)),
        pl.BlockSpec((1,) + plane, lambda i: (here(i), 0, 0)),
        pl.BlockSpec((1,) + plane, lambda i: (here(i), 0, 0)),
        pl.BlockSpec((3 * LANES, LANES), lambda i: (0, 0)),
        pl.BlockSpec((width, 3 * width), lambda i: (0, 0)),
    ]
    inputs = [flags, potential, potential, ahead_t, multiplier, start, final, *tables]
    aliases = {}
    if not lead:
        in_specs.append(pl.BlockSpec((steps,) + plane, lambda i: (0, 0, 0)))
        inputs.append(fx_in)
    if first_row + count == rows:
        in_specs.append(pl.BlockSpec((steps, 1) + plane, lambda i: (0, 0, 0, 0)))
        inputs.append(ahead_x)
    if nm is not None:
        in_specs.append(pl.BlockSpec(memory_space=pl.ANY))
        aliases = {len(inputs): 0}
        inputs.append(nm)
    f32 = jnp.float32
    cells = count * steps * width * LANES
    return pl.pallas_call(
        lambda *refs: pointwise_kernel(len(inputs), first_row, lead, count, rows, steps, n_tm, *refs),
        grid=(lead + count,),
        in_specs=in_specs,
        out_specs=[
            pl.BlockSpec((4, steps, 1) + plane, lambda i: (0, 0, first_row + slot(i), 0, 0)),
            pl.BlockSpec((steps,) + plane, lambda i: (0, 0, 0)),
        ]
        + [pl.BlockSpec((steps + 1, 1, block, LANES), lambda i: (0, slot(i), 0, 0))] * n_tm,
        out_shape=[
            jax.ShapeDtypeStruct(multiplier.shape, f32),
            jax.ShapeDtypeStruct((steps,) + plane, f32),
        ]
        + [jax.ShapeDtypeStruct((steps + 1, count, block, LANES), f32)] * n_tm,
        scratch_shapes=[
            pltpu.VMEM((steps + 1,) + plane, f32),
            pltpu.VMEM((steps,) + plane, f32),
            pltpu.VMEM(plane, f32),
            pltpu.VMEM((width + GROUP, LANES), f32),
        ],
        input_output_aliases=aliases,
        compiler_params=params(),
        cost_estimate=cost(cells * (lead + count) // count, 36),
        name="pointwise",
    )(*inputs)


def time_kernel(steps, n_sp, spot, *refs):
    t_all, stage = refs[-2:]
    got, out = refs[: -2 - n_sp], refs[-2 - n_sp : -2]
    n = len(got)
    me_t, me_x = spot[0, 0], spot[0, 1]
    total = n * steps
    share = total // n_sp

    def group(i, carry):
        at = pl.ds(pl.multiple_of(i * GROUP, GROUP), GROUP)
        for d in range(n):
            s = me_t ^ d
            t_all[s, pl.ds(0, steps + 1)] = got[d][:, 0, at, :]
        xs = [t_all[b, t] for b in range(n) for t in range(steps)]
        for b in range(n - 1):
            flux = t_all[b, steps]
            xs[(b + 1) * steps - 1] = xs[(b + 1) * steps - 1] + flux
            xs[(b + 1) * steps] = xs[(b + 1) * steps] - flux
        for k, v in enumerate(dct(xs)):
            stage[(k // share) ^ me_x, k % share] = v
        for d in range(n_sp):
            out[d][:, 0, at, :] = stage[d]
        return carry

    lax.fori_loop(0, got[0].shape[2] // GROUP, group, 0)


def time_transform(spot, got, n_sp):
    planes, count, block, lanes = got[0].shape
    n = len(got)
    share = n * (planes - 1) // n_sp
    return pl.pallas_call(
        lambda *refs: time_kernel(planes - 1, n_sp, *refs),
        grid=(count,),
        in_specs=[pl.BlockSpec(memory_space=pltpu.SMEM)]
        + [pl.BlockSpec((planes, 1, block, lanes), lambda i: (0, i, 0, 0))] * n,
        out_specs=[pl.BlockSpec((share, 1, block, lanes), lambda i: (0, i, 0, 0))] * n_sp,
        out_shape=[jax.ShapeDtypeStruct((share, count, block, lanes), jnp.float32)] * n_sp,
        scratch_shapes=[
            pltpu.VMEM((n, planes, GROUP, lanes), jnp.float32),
            pltpu.VMEM((n_sp, share, GROUP, lanes), jnp.float32),
        ],
        compiler_params=params(),
        cost_estimate=cost(got[0].size * n, 10),
        name="time",
    )(spot, *got)


def middle_kernel(n_sp, first_rows, spot, sig, *refs):
    x_all, stage = refs[-2:]
    got, out = refs[: -2 - n_sp], refs[-2 - n_sp : -2]
    me = spot[0, 1]
    share, count = got[0].shape[:2]
    rows = count * len(first_rows)
    eig = RATE * eigen(rows * n_sp)

    def one(k, carry):
        for c, first in enumerate(first_rows):
            for d in range(n_sp):
                for r in range(count):
                    x_all[d ^ me, first + r] = got[c * n_sp + d][k, r]
        xs = dct([x_all[j, r] for j in range(n_sp) for r in range(rows)])
        base = sig[k]
        xs = [x * refined(base + float(eig[i])) for i, x in enumerate(xs)]
        for x, v in enumerate(dct(xs)):
            stage[(x // rows) ^ me, x % rows] = v
        for d in range(n_sp):
            out[d][k] = stage[d]
        return carry

    lax.fori_loop(0, share, one, 0)


def middle(g, spot, sig, got, first_rows, n_sp):
    share, count, block, lanes = got[0].shape
    rows = count * len(first_rows)
    f32 = jnp.float32
    size = n_sp * share * rows * GROUP * lanes
    return pl.pallas_call(
        lambda *refs: middle_kernel(n_sp, first_rows, *refs),
        grid=(1,),
        in_specs=[
            pl.BlockSpec(memory_space=pltpu.SMEM),
            pl.BlockSpec((share, GROUP, lanes), lambda i: (0, g, 0)),
        ]
        + [pl.BlockSpec((share, count, GROUP, lanes), lambda i: (0, 0, g, 0))] * len(got),
        out_specs=[pl.BlockSpec((share, rows, GROUP, lanes), lambda i: (0, 0, 0, 0))] * n_sp,
        out_shape=[jax.ShapeDtypeStruct((share, rows, GROUP, lanes), f32)] * n_sp,
        scratch_shapes=[pltpu.VMEM((n_sp, rows, GROUP, lanes), f32)] * 2,
        compiler_params=params(),
        cost_estimate=cost(size, 18),
        name="middle",
    )(spot, sig, *got)


def untime_kernel(steps, n_tm, spot, *refs):
    k_all, stage = refs[-2:]
    got, out = refs[: -2 - n_tm], refs[-2 - n_tm : -2]
    me_t, me_x = spot[0, 0], spot[0, 1]
    share, rows = got[0].shape[:2]

    def one(r, carry):
        for d in range(len(got)):
            k_all[d ^ me_x] = got[d][:, r]
        xs = dct([k_all[j, k] for j in range(len(got)) for k in range(share)])
        for t, v in enumerate(xs):
            stage[(t // steps) ^ me_t, t % steps] = v
        for d in range(n_tm):
            out[d][:, r] = stage[d]
        return carry

    lax.fori_loop(0, rows, one, 0)


def untime(spot, got, n_tm):
    share, rows, group, lanes = got[0].shape
    steps = share * len(got) // n_tm
    f32 = jnp.float32
    size = n_tm * steps * rows * group * lanes
    return pl.pallas_call(
        lambda *refs: untime_kernel(steps, n_tm, *refs),
        grid=(1,),
        in_specs=[pl.BlockSpec(memory_space=pltpu.SMEM)]
        + [pl.BlockSpec(got[0].shape, lambda i: (0, 0, 0, 0))] * len(got),
        out_specs=[pl.BlockSpec((steps, rows, group, lanes), lambda i: (0, 0, 0, 0))] * n_tm,
        out_shape=[jax.ShapeDtypeStruct((steps, rows, group, lanes), f32)] * n_tm,
        scratch_shapes=[
            pltpu.VMEM((len(got), share, group, lanes), f32),
            pltpu.VMEM((n_tm, steps, group, lanes), f32),
        ],
        compiler_params=params(),
        cost_estimate=cost(size, 11),
        name="untime",
    )(spot, *got)


def back_kernel(*refs):
    got, (cy, cz, out, whole) = refs[:-4], refs[-4:]
    for t in range(out.shape[0]):
        for n, part in enumerate(got):
            whole[t, pl.ds(n * GROUP, GROUP), :] = part[t, 0]

    batch = min(BATCH, out.shape[0])

    def some(b, carry):
        planes = [whole[b * batch + k] for k in range(batch)]
        for k, full in enumerate(plane_mm(planes, cy[...], cz[...])):
            out[b * batch + k, 0] = full
        return carry

    lax.fori_loop(0, out.shape[0] // batch, some, 0)


def back(got, cy, cz):
    steps, rows, group, lanes = got[0].shape
    width = group * len(got)
    return pl.pallas_call(
        back_kernel,
        grid=(rows,),
        in_specs=[pl.BlockSpec((steps, 1, group, lanes), lambda i: (0, i, 0, 0))] * len(got)
        + [
            pl.BlockSpec((width, 3 * width), lambda i: (0, 0)),
            pl.BlockSpec((3 * lanes, lanes), lambda i: (0, 0)),
        ],
        out_specs=pl.BlockSpec((steps, 1, width, lanes), lambda i: (0, i, 0, 0)),
        out_shape=jax.ShapeDtypeStruct((steps, rows, width, lanes), jnp.float32),
        scratch_shapes=[pltpu.VMEM((steps, width, lanes), jnp.float32)],
        compiler_params=params(),
        cost_estimate=cost(steps * rows * width * lanes, 7),
        name="back",
    )(*got, cy, cz)


def from_behind(block, axis, distance):
    devices = range(lax.axis_size(axis))
    route = [(i - distance, i) for i in devices if i - distance in devices]
    return lax.ppermute(block, axis, route)


def trade(parts, axis):
    devices = range(lax.axis_size(axis))
    return [parts[0]] + [
        lax.ppermute(parts[d], axis, [(i, i ^ d) for i in devices]) for d in range(1, len(parts))
    ]


def body(potential, multiplier, start_density, final_density):
    steps, rows, width, lanes = potential.shape
    n_tm = lax.axis_size("tm")
    n_sp = lax.axis_size("space")
    me_t = lax.axis_index("tm")
    me_x = lax.axis_index("space")
    total_t = steps * n_tm
    block = width // n_tm
    groups = block // GROUP
    share = total_t // n_sp
    parts = min(rows, 4)
    count = rows // parts
    f32 = jnp.float32
    ahead_t = from_behind(potential[:1], "tm", -1)
    ahead_x = from_behind(potential[:, :1], "space", -1)
    flags = jnp.stack(
        [me_t < n_tm - 1, me_x < n_sp - 1, me_t == 0, me_t == n_tm - 1]
    ).astype(f32)[None]
    spot = jnp.stack([me_t, me_x]).astype(jnp.int32)[None]

    cos_y = thirds(cosine_table(width))
    to = me_t ^ jnp.arange(n_tm)
    rows_y = cos_y.reshape(3, n_tm, block, width)[:, to].reshape(3, width, width)
    rows_y = rows_y.transpose(1, 0, 2).reshape(width, 3 * width)
    columns_y = cos_y.reshape(3, width, n_tm, groups, GROUP)[:, :, to]
    columns_y = columns_y.transpose(1, 0, 3, 2, 4).reshape(width, 3 * width)
    cos_z = thirds(cosine_table(lanes).T).reshape(3 * lanes, lanes)
    tables = (cos_z, rows_y)

    eig_t = jnp.asarray(eigen(total_t), f32)
    eig_t = lax.dynamic_slice_in_dim(eig_t, me_x * share, share, 0)[:, None, None]
    eig_yz = jnp.asarray(eigen(width)[:, None] + eigen(lanes)[None, :], f32)
    eig_yz = lax.dynamic_slice_in_dim(eig_yz, me_t * block, block, 0)[None]
    sig = RATE * (eig_t + eig_yz) + PROX

    operands = (flags, potential, multiplier, start_density, final_density, ahead_t, ahead_x)
    flux, next_multiplier = None, None
    moved, first_rows = [], []
    for n in range(parts):
        first = ((n + 1) % parts) * count
        if first == 0:
            flux = from_behind(flux, "space", 1)
        next_multiplier, flux, *pay = pointwise(
            first, 1 if n == 0 else 0, count, n_tm, operands, tables, flux, next_multiplier
        )
        timed = time_transform(spot, trade(pay, "tm"), n_sp)
        moved += trade(timed, "space")
        first_rows.append(first)
    final = []
    for g in range(groups):
        solved = middle(g, spot, sig, moved, first_rows, n_sp)
        solved = trade(solved, "space")
        steps_of = untime(spot, solved, n_tm)
        final += trade(steps_of, "tm")
    next_potential = back(final, columns_y, cos_z)
    return (next_potential, next_multiplier)


def solution(mesh):
    in_specs = (
        P("tm", "space", None, None),
        P(None, "tm", "space", None, None),
        P("space", None, None),
        P("space", None, None),
    )
    out_specs = (P("tm", "space", None, None), P(None, "tm", "space", None, None))
    return jax.shard_map(body, mesh=mesh, in_specs=in_specs, out_specs=out_specs, check_vma=False)
```

time: 1030 us -> 615 us (0.60)
  blocking collectives: 383 us -> 0 us
  other arithmetic: 199 us -> 1.91 us
  Pallas kernels: 0 us -> 192 us
  starting transfers between devices: 16.9 us -> 176 us
  matrix products: 136 us -> 0 us
  local copies, waits for them, and re-layouts: 101 us -> 10.9 us
  waiting for transfers between devices: 188 us -> 224 us
    all_to_all x3 -> x0, blocking collectives: 383 us -> none  [the longest x1 188 us: body(): lax.all_to_all(solved, 'space', split_axis=1, concat_axis=2, tiled=True)]
    ppermute x0 -> x80, waiting for transfers between devices: none -> 215 us  [trade(): lax.ppermute(parts[d], axis, [(i, i ^ d) for i in devices])]
    pallas_call x0 -> x17, Pallas kernels: none -> 192 us  [the longest x4 86.6 us: pointwise(): pl.pallas_call(lambda *refs: pointwise_kernel(len(inputs), first_row, lea...]
    all_to_all x1 -> x0, waiting for transfers between devices: 183 us -> none  [body(): lax.all_to_all(lax.all_to_all(payload, 'tm', split_axis=3, concat_axis=1,...]
    ppermute x0 -> x80, starting transfers between devices: none -> 171 us  [trade(): lax.ppermute(parts[d], axis, [(i, i ^ d) for i in devices])]
    dot_general x8 -> x0, matrix products: 136 us -> none  [the longest x1 28.1 us: body(): payload = jnp.einsum('ctxyi,ki->ctxyk', payload, cos_z, precision=high)]
    sub x3 -> x0, other arithmetic: 77 us -> none  [the longest x1 53.1 us: body(): flux = next_multiplier - RATE * projected]
    select_n x2 -> x1, other arithmetic: 61.5 us -> 0.01 us  [body(): cos_y.reshape(3, n_tm, block, width)[:, to].reshape(3, width, width)]
  transfers between devices with their start and end apart: 5 -> 83, of which waited for: 2 -> 26; matrix products, arithmetic and copies ran while one was open for 6% -> 1% of each run, Pallas kernels for 0% -> 28%
where the time goes in v1:
time: 615 us; the launch traced here: 607 us
  waiting for transfers between devices  224 us (36%)
  Pallas kernels  192 us (31%)
  starting transfers between devices  176 us (29%)
  local copies, waits for them, and re-layouts  10.9 us (2%)
    ppermute x80, waiting for transfers between devices, trade(): lax.ppermute(parts[d], axis, [(i, i ^ d) for i in devices])  215 us
    ppermute x80, starting transfers between devices, trade(): lax.ppermute(parts[d], axis, [(i, i ^ d) for i in devices])  171 us
    pallas_call x4, Pallas kernels, pointwise(): pl.pallas_call(lambda *refs: pointwise_kernel(len(inputs), first_row, lea...  86.6 us
    pallas_call x4, Pallas kernels, middle(): pl.pallas_call(lambda *refs: middle_kernel(n_sp, first_rows, *refs), grid...  40.1 us
    pallas_call x4, Pallas kernels, untime(): pl.pallas_call(lambda *refs: untime_kernel(steps, n_tm, *refs), grid=(1,)...  26.6 us
    pallas_call x4, Pallas kernels, time_transform(): pl.pallas_call(lambda *refs: time_kernel(planes - 1, n_sp, *refs), grid=(...  25 us
    pallas_call x1, Pallas kernels, back(): pl.pallas_call(back_kernel, grid=(rows,), in_specs=[pl.BlockSpec((steps,...  13.9 us
  transfers between devices with their start and end apart: 83, of which 26 were waited for; matrix products, arithmetic and copies ran while one was open for 1% of the time, Pallas kernels for 28%

profile of v1, /device:TPU:0, one launch (start us, length us, event | category | flops | bytes accessed | tf_op | source)
XLA Modules:
  0.0 607.1 jit_solution(2663931409780312538)
XLA Ops:
  9.2 9.3 %collective-permute-done.refs_3_ = f32[1,8,128,128]{3,2,1,0:T(8,128)S(1)} collective-permute-done((f32[1,8,128,128]{3,2,1,0:T(8,128)S(1)}, f32[1,8,128,128]{3,2,1,0:T(8,128)S(1)}, u32[]{:S(2)}, u32[]{:S(2)}) %collective-permute-start) | collective-permute-done | bytes 524320 | tf_op jit(solution)/shard_map/ppermute | solution.py:444
  19.3 26.3 %pointwise.4 = (f32[4,16,8,128,128]{4,3,2,1,0:T(8,128)}, f32[16,128,128]{2,1,0:T(8,128)}, f32[17,2,32,128]{3,2,1,0:T(8,128)}, f32[17,2,32,128]{3,2,1,0:T(8,128)}...) custom-call(f32[1,4]{1,0:T(1,128)} %add_convert_fusion.refs_0_, f32[16,8,128,128]{3,2,1,0:T(8,128)} %refs_2_.7, ...), custom_call_target="tpu_custom_call" | custom-call | flops 32558284800 | tf_op jit(solution)/shard_map/pointwise/pallas_call | solution.py:241
  49.8 19.9 %pointwise.5 = (f32[4,16,8,128,128]{4,3,2,1,0:T(8,128)}, f32[16,128,128]{2,1,0:T(8,128)}, f32[17,2,32,128]{3,2,1,0:T(8,128)}, f32[17,2,32,128]{3,2,1,0:T(8,128)}...) custom-call(f32[1,4]{1,0:T(1,128)} %add_convert_fusion.refs_0_, ...), custom_call_target="tpu_custom_call", output_to_operand_aliasing={{0}: (10, {})} | custom-call | flops 21705523200 | tf_op jit(solution)/shard_map/pointwise/pallas_call | solution.py:241
  82.3 20.6 %pointwise.6 = (f32[4,16,8,128,128]{4,3,2,1,0:T(8,128)}, f32[16,128,128]{2,1,0:T(8,128)}, f32[17,2,32,128]{3,2,1,0:T(8,128)}, f32[17,2,32,128]{3,2,1,0:T(8,128)}...) custom-call(f32[1,4]{1,0:T(1,128)} %add_convert_fusion.refs_0_, ...), custom_call_target="tpu_custom_call", output_to_operand_aliasing={{0}: (11, {})} | custom-call | flops 21705523200 | tf_op jit(solution)/shard_map/pointwise/pallas_call | solution.py:241
  117.4 7.8 %collective-permute-done.5.refs_4_ = f32[8,2,32,128]{3,2,1,0:T(8,128)S(1)} collective-permute-done((f32[8,2,32,128]{3,2,1,0:T(8,128)S(1)}, f32[8,2,32,128]{3,2,1,0:T(8,128)S(1)}, u32[]{:S(2)}, u32[]{:S(2)}) %collective-permute-start.5) | collective-permute-done | bytes 262176 | tf_op jit(solution)/shard_map/ppermute | solution.py:450
  131.0 11.0 %collective-permute-start.10 = (f32[8,2,32,128]{3,2,1,0:T(8,128)S(1)}, f32[8,2,32,128]{3,2,1,0:T(8,128)S(1)}, u32[]{:S(2)}, u32[]{:S(2)}) collective-permute-start(f32[8,2,32,128]{3,2,1,0:T(8,128)S(1)} %copy-done.79), channel_id=1, source_target_pairs={{0,7},{1,6},{2,5},{3,4},{4,3},{5,2},{6,1},{7,0},{8,15},{9,14},{10,... | collective-permute-start | bytes 786440 | tf_op jit(solution)/shard_map/ppermute | solution.py:450
  154.6 12.6 %collective-permute-start.16 = (f32[8,2,32,128]{3,2,1,0:T(8,128)}, f32[8,2,32,128]{3,2,1,0:T(8,128)S(1)}, u32[]{:S(2)}, u32[]{:S(2)}) collective-permute-start(f32[8,2,32,128]{3,2,1,0:T(8,128)} %get-tuple-element.126), channel_id=1, source_target_pairs={{0,3},{1,2},{2,1},{3,0},{4,7},{5,6},{6,5},{7,4},{8,11},{9,10},{10,... | collective-permute-start | bytes 786440 | tf_op jit(solution)/shard_map/ppermute | solution.py:450
  169.8 19.8 %pointwise.7 = (f32[4,16,8,128,128]{4,3,2,1,0:T(8,128)}, f32[16,128,128]{2,1,0:T(8,128)}, f32[17,2,32,128]{3,2,1,0:T(8,128)}, f32[17,2,32,128]{3,2,1,0:T(8,128)}...) custom-call(f32[1,4]{1,0:T(1,128)} %add_convert_fusion.refs_0_, ...), custom_call_target="tpu_custom_call", output_to_operand_aliasing={{0}: (10, {})} | custom-call | flops 21705523200 | tf_op jit(solution)/shard_map/pointwise/pallas_call | solution.py:241
  211.9 9.8 %collective-permute-start.26 = (f32[8,2,32,128]{3,2,1,0:T(8,128)}, f32[8,2,32,128]{3,2,1,0:T(8,128)}, u32[]{:S(2)}, u32[]{:S(2)}) collective-permute-start(f32[8,2,32,128]{3,2,1,0:T(8,128)} %get-tuple-element.139), channel_id=1, source_target_pairs={{0,2},{1,3},{2,0},{3,1},{4,6},{5,7},{6,4},{7,5},{8,10},{9,11},{10,... | collective-permute-start | bytes 786440 | tf_op jit(solution)/shard_map/ppermute | solution.py:450
  243.4 19.5 %collective-permute-done.29.refs_23_ = f32[8,2,32,128]{3,2,1,0:T(8,128)} collective-permute-done((f32[8,2,32,128]{3,2,1,0:T(8,128)}, f32[8,2,32,128]{3,2,1,0:T(8,128)}, u32[]{:S(2)}, u32[]{:S(2)}) %collective-permute-start.29) | collective-permute-done | bytes 262176 | tf_op jit(solution)/shard_map/ppermute | solution.py:450
  269.4 10.7 %collective-permute-start.40 = (f32[8,2,32,128]{3,2,1,0:T(8,128)}, f32[8,2,32,128]{3,2,1,0:T(8,128)}, u32[]{:S(2)}, u32[]{:S(2)}) collective-permute-start(f32[8,2,32,128]{3,2,1,0:T(8,128)} %get-tuple-element.156), channel_id=1, source_target_pairs={{0,5},{1,4},{2,7},{3,6},{4,1},{5,0},{6,3},{7,2},{8,13},{9,12},{10,... | collective-permute-start | bytes 786440 | tf_op jit(solution)/shard_map/ppermute | solution.py:450
  284.9 17.6 %collective-permute-done.39.refs_30_ = f32[8,2,32,128]{3,2,1,0:T(8,128)} collective-permute-done((f32[8,2,32,128]{3,2,1,0:T(8,128)}, f32[8,2,32,128]{3,2,1,0:T(8,128)}, u32[]{:S(2)}, u32[]{:S(2)}) %collective-permute-start.39) | collective-permute-done | bytes 262176 | tf_op jit(solution)/shard_map/ppermute | solution.py:450
  307.9 10.1 %middle.4 = (f32[8,8,8,128]{3,2,1,0:T(8,128)}, f32[8,8,8,128]{3,2,1,0:T(8,128)}, f32[8,8,8,128]{3,2,1,0:T(8,128)}, f32[8,8,8,128]{3,2,1,0:T(8,128)}, f32[8,8,8,1...) custom-call(s32[1,2]{1,0:T(1,128)} %add_bitcast_fusion.refs_0_, ...), custom_call_target="tpu_custom_call" | custom-call | flops 10852761600 | tf_op jit(solution)/shard_map/middle/pallas_call | solution.py:346
  318.4 11.6 %collective-permute-start.44 = (f32[8,8,8,128]{3,2,1,0:T(8,128)}, f32[8,8,8,128]{3,2,1,0:T(8,128)S(1)}, u32[]{:S(2)}, u32[]{:S(2)}) collective-permute-start(f32[8,8,8,128]{3,2,1,0:T(8,128)} %get-tuple-element.161), channel_id=1, source_target_pairs={{0,2},{1,3},{2,0},{3,1},{4,6},{5,7},{6,4},{7,5},{8,10},{9,11},{10,... | collective-permute-start | bytes 786440 | tf_op jit(solution)/shard_map/ppermute | solution.py:450
  332.4 10.0 %middle.5 = (f32[8,8,8,128]{3,2,1,0:T(8,128)}, f32[8,8,8,128]{3,2,1,0:T(8,128)}, f32[8,8,8,128]{3,2,1,0:T(8,128)}, f32[8,8,8,128]{3,2,1,0:T(8,128)}, f32[8,8,8,1...) custom-call(s32[1,2]{1,0:T(1,128)} %add_bitcast_fusion.refs_0_, ...), custom_call_target="tpu_custom_call" | custom-call | flops 10852761600 | tf_op jit(solution)/shard_map/middle/pallas_call | solution.py:346
  352.8 14.1 %collective-permute-done.47.refs_6_ = f32[8,8,8,128]{3,2,1,0:T(8,128)S(1)} collective-permute-done((f32[8,8,8,128]{3,2,1,0:T(8,128)}, f32[8,8,8,128]{3,2,1,0:T(8,128)S(1)}, u32[]{:S(2)}, u32[]{:S(2)}) %collective-permute-start.47) | collective-permute-done | bytes 262176 | tf_op jit(solution)/shard_map/ppermute | solution.py:450
  366.9 10.0 %middle.6 = (f32[8,8,8,128]{3,2,1,0:T(8,128)}, f32[8,8,8,128]{3,2,1,0:T(8,128)}, f32[8,8,8,128]{3,2,1,0:T(8,128)}, f32[8,8,8,128]{3,2,1,0:T(8,128)}, f32[8,8,8,1...) custom-call(s32[1,2]{1,0:T(1,128)} %add_bitcast_fusion.refs_0_, ...), custom_call_target="tpu_custom_call" | custom-call | flops 10852761600 | tf_op jit(solution)/shard_map/middle/pallas_call | solution.py:346
  384.8 9.9 %middle.7 = (f32[8,8,8,128]{3,2,1,0:T(8,128)}, f32[8,8,8,128]{3,2,1,0:T(8,128)}, f32[8,8,8,128]{3,2,1,0:T(8,128)}, f32[8,8,8,128]{3,2,1,0:T(8,128)}, f32[8,8,8,1...) custom-call(s32[1,2]{1,0:T(1,128)} %add_bitcast_fusion.refs_0_, ...), custom_call_target="tpu_custom_call" | custom-call | flops 10852761600 | tf_op jit(solution)/shard_map/middle/pallas_call | solution.py:346
  394.8 14.4 %collective-permute-done.56.refs_5_ = f32[8,8,8,128]{3,2,1,0:T(8,128)S(1)} collective-permute-done((f32[8,8,8,128]{3,2,1,0:T(8,128)S(1)}, f32[8,8,8,128]{3,2,1,0:T(8,128)S(1)}, u32[]{:S(2)}, u32[]{:S(2)}) %collective-permute-start.56) | collective-permute-done | bytes 262176 | tf_op jit(solution)/shard_map/ppermute | solution.py:450
  415.6 6.7 %collective-permute-start.66 = (f32[8,8,8,128]{3,2,1,0:T(8,128)S(1)}, f32[8,8,8,128]{3,2,1,0:T(8,128)S(1)}, u32[]{:S(2)}, u32[]{:S(2)}) collective-permute-start(f32[8,8,8,128]{3,2,1,0:T(8,128)S(1)} %copy-done.61), channel_id=1, source_target_pairs={{0,4},{1,5},{2,6},{3,7},{4,0},{5,1},{6,2},{7,3},{8,12},{9,13},{10,... | collective-permute-start | bytes 786440 | tf_op jit(solution)/shard_map/ppermute | solution.py:450
  422.4 10.7 %collective-permute-start.67 = (f32[8,8,8,128]{3,2,1,0:T(8,128)S(1)}, f32[8,8,8,128]{3,2,1,0:T(8,128)S(1)}, u32[]{:S(2)}, u32[]{:S(2)}) collective-permute-start(f32[8,8,8,128]{3,2,1,0:T(8,128)S(1)} %copy-done.58), channel_id=1, source_target_pairs={{0,5},{1,4},{2,7},{3,6},{4,1},{5,0},{6,3},{7,2},{8,13},{9,12},{10,... | collective-permute-start | bytes 786440 | tf_op jit(solution)/shard_map/ppermute | solution.py:450
  443.8 10.5 %collective-permute-done.66.refs_5_ = f32[8,8,8,128]{3,2,1,0:T(8,128)S(1)} collective-permute-done((f32[8,8,8,128]{3,2,1,0:T(8,128)S(1)}, f32[8,8,8,128]{3,2,1,0:T(8,128)S(1)}, u32[]{:S(2)}, u32[]{:S(2)}) %collective-permute-start.66) | collective-permute-done | bytes 262176 | tf_op jit(solution)/shard_map/ppermute | solution.py:450
  460.6 6.7 %collective-permute-start.76 = (f32[8,8,8,128]{3,2,1,0:T(8,128)}, f32[8,8,8,128]{3,2,1,0:T(8,128)S(1)}, u32[]{:S(2)}, u32[]{:S(2)}) collective-permute-start(f32[8,8,8,128]{3,2,1,0:T(8,128)} %get-tuple-element.199), channel_id=1, source_target_pairs={{0,4},{1,5},{2,6},{3,7},{4,0},{5,1},{6,2},{7,3},{8,12},{9,13},{10,... | collective-permute-start | bytes 786440 | tf_op jit(solution)/shard_map/ppermute | solution.py:450
  467.4 6.6 %untime.5 = (f32[16,8,8,128]{3,2,1,0:T(8,128)}, f32[16,8,8,128]{3,2,1,0:T(8,128)}, f32[16,8,8,128]{3,2,1,0:T(8,128)}, f32[16,8,8,128]{3,2,1,0:T(8,128)}) custom-call(s32[1,2]{1,0:T(1,128)} %add_bitcast_fusion.refs_0_, f32[8,8,8,128]{3,2,1,0:T(8,128)} %get-tuple-element.171.refs_1_, f32[8,8,8,128]{3,2,1,0:T(8,128)} %copy-done.40, ...), custom_call_target="tpu_custom_call" | custom-call | flops 6632243200 | tf_op jit(solution)/shard_map/untime/pallas_call | solution.py:387
  481.8 17.4 %collective-permute-done.76.refs_5_ = f32[8,8,8,128]{3,2,1,0:T(8,128)S(1)} collective-permute-done((f32[8,8,8,128]{3,2,1,0:T(8,128)}, f32[8,8,8,128]{3,2,1,0:T(8,128)S(1)}, u32[]{:S(2)}, u32[]{:S(2)}) %collective-permute-start.76) | collective-permute-done | bytes 262176 | tf_op jit(solution)/shard_map/ppermute | solution.py:450
  501.4 6.7 %untime.6 = (f32[16,8,8,128]{3,2,1,0:T(8,128)}, f32[16,8,8,128]{3,2,1,0:T(8,128)}, f32[16,8,8,128]{3,2,1,0:T(8,128)}, f32[16,8,8,128]{3,2,1,0:T(8,128)}) custom-call(s32[1,2]{1,0:T(1,128)} %add_bitcast_fusion.refs_0_, f32[8,8,8,128]{3,2,1,0:T(8,128)} %get-tuple-element.183.refs_1_, f32[8,8,8,128]{3,2,1,0:T(8,128)} %copy-done.48, ...), custom_call_target="tpu_custom_call" | custom-call | flops 6632243200 | tf_op jit(solution)/shard_map/untime/pallas_call | solution.py:387
  512.1 13.5 %collective-permute-done.51.refs_2_ = f32[16,8,8,128]{3,2,1,0:T(8,128)S(1)} collective-permute-done((f32[16,8,8,128]{3,2,1,0:T(8,128)}, f32[16,8,8,128]{3,2,1,0:T(8,128)S(1)}, u32[]{:S(2)}, u32[]{:S(2)}) %collective-permute-start.51) | collective-permute-done | bytes 524320 | tf_op jit(solution)/shard_map/ppermute | solution.py:450
  536.0 12.1 %collective-permute-done.61.refs_6_ = f32[16,8,8,128]{3,2,1,0:T(8,128)S(1)} collective-permute-done((f32[16,8,8,128]{3,2,1,0:T(8,128)}, f32[16,8,8,128]{3,2,1,0:T(8,128)S(1)}, u32[]{:S(2)}, u32[]{:S(2)}) %collective-permute-start.61) | collective-permute-done | bytes 524320 | tf_op jit(solution)/shard_map/ppermute | solution.py:450
  560.8 9.8 %collective-permute-done.71.refs_10_ = f32[16,8,8,128]{3,2,1,0:T(8,128)} collective-permute-done((f32[16,8,8,128]{3,2,1,0:T(8,128)}, f32[16,8,8,128]{3,2,1,0:T(8,128)}, u32[]{:S(2)}, u32[]{:S(2)}) %collective-permute-start.71) | collective-permute-done | bytes 524320 | tf_op jit(solution)/shard_map/ppermute | solution.py:450
  570.7 8.2 %collective-permute-done.80.refs_13_ = f32[16,8,8,128]{3,2,1,0:T(8,128)} collective-permute-done((f32[16,8,8,128]{3,2,1,0:T(8,128)}, f32[16,8,8,128]{3,2,1,0:T(8,128)}, u32[]{:S(2)}, u32[]{:S(2)}) %collective-permute-start.80) | collective-permute-done | bytes 524320 | tf_op jit(solution)/shard_map/ppermute | solution.py:450
  578.9 14.1 %collective-permute-done.81.refs_14_ = f32[16,8,8,128]{3,2,1,0:T(8,128)} collective-permute-done((f32[16,8,8,128]{3,2,1,0:T(8,128)}, f32[16,8,8,128]{3,2,1,0:T(8,128)}, u32[]{:S(2)}, u32[]{:S(2)}) %collective-permute-start.81) | collective-permute-done | bytes 524320 | tf_op jit(solution)/shard_map/ppermute | solution.py:450
  593.0 13.9 %back.1 = f32[16,8,128,128]{3,2,1,0:T(8,128)} custom-call(f32[16,8,8,128]{3,2,1,0:T(8,128)} %get-tuple-element.167.refs_0_, f32[16,8,8,128]{3,2,1,0:T(8,128)} %copy-done.18, f32[16,8,8,128]{3,2,1,0:T(8,128)} %copy-done.19, f32[16,8,8,128]{3,2,1,0:T(8,128)} %copy-done.20, f32[16,8,8,128]{3,2,1,0:T(8,128)} %get-tuple-element.179.refs_4_, ...), custom_call_target="tpu_custom_call" | custom-call | flops 16882073600 | tf_op jit(solution)/shard_map/back/pallas_call | solution.py:424
  (351 shorter events, 203.2 us)
Async XLA Ops:
  4.3 77.0 %collective-permute-start.21 = (f32[16,1,128,128]{3,2,1,0:T(8,128)S(1)}, f32[16,1,128,128]{3,2,1,0:T(8,128)S(1)}, u32[]{:S(2)}, u32[]{:S(2)}) collective-permute-start(f32[16,1,128,128]{3,2,1,0:T(8,128)S(1)} %slice.7), channel_id=1, source_target_pairs={{1,0},{2,1},{3,2},{4,3},{5,4},{6,5},{7,6},{9,8},{10,9},{11,10},{12... | collective-permute-start | bytes 3145736 | tf_op jit(solution)/shard_map/ppermute | solution.py:444
  69.7 35.7 %collective-permute-start.11 = (f32[17,2,32,128]{3,2,1,0:T(8,128)}, f32[17,2,32,128]{3,2,1,0:T(8,128)S(1)}, u32[]{:S(2)}, u32[]{:S(2)}) collective-permute-start(f32[17,2,32,128]{3,2,1,0:T(8,128)} %get-tuple-element.120), channel_id=1, source_target_pairs={{0,8},{8,0},{16,24},{24,16},{1,9},{9,1},{17,25},{25,17},{2,10},{10... | collective-permute-start | bytes 1671176 | tf_op jit(solution)/shard_map/ppermute | solution.py:450
  71.7 35.3 %collective-permute-start.12 = (f32[17,2,32,128]{3,2,1,0:T(8,128)}, f32[17,2,32,128]{3,2,1,0:T(8,128)S(1)}, u32[]{:S(2)}, u32[]{:S(2)}) collective-permute-start(f32[17,2,32,128]{3,2,1,0:T(8,128)} %get-tuple-element.121), channel_id=1, source_target_pairs={{0,16},{8,24},{16,0},{24,8},{1,17},{9,25},{17,1},{25,9},{2,18},{10... | collective-permute-start | bytes 1671176 | tf_op jit(solution)/shard_map/ppermute | solution.py:450
  103.0 64.2 %collective-permute-start.32 = (f32[16,128,128]{2,1,0:T(8,128)}, f32[16,128,128]{2,1,0:T(8,128)S(1)}, u32[]{:S(2)}, u32[]{:S(2)}) collective-permute-start(f32[16,128,128]{2,1,0:T(8,128)} %get-tuple-element.145), channel_id=1, source_target_pairs={{0,1},{1,2},{2,3},{3,4},{4,5},{5,6},{6,7},{8,9},{9,10},{10,11},{11... | collective-permute-start | bytes 3145736 | tf_op jit(solution)/shard_map/ppermute | solution.py:444
  108.1 34.0 %collective-permute-start.7 = (f32[8,2,32,128]{3,2,1,0:T(8,128)S(1)}, f32[8,2,32,128]{3,2,1,0:T(8,128)S(1)}, u32[]{:S(2)}, u32[]{:S(2)}) collective-permute-start(f32[8,2,32,128]{3,2,1,0:T(8,128)S(1)} %copy-done.84), channel_id=1, source_target_pairs={{0,4},{1,5},{2,6},{3,7},{4,0},{5,1},{6,2},{7,3},{8,12},{9,13},{10,... | collective-permute-start | bytes 786440 | tf_op jit(solution)/shard_map/ppermute | solution.py:450
  110.8 34.7 %collective-permute-start.8 = (f32[8,2,32,128]{3,2,1,0:T(8,128)S(1)}, f32[8,2,32,128]{3,2,1,0:T(8,128)S(1)}, u32[]{:S(2)}, u32[]{:S(2)}) collective-permute-start(f32[8,2,32,128]{3,2,1,0:T(8,128)S(1)} %copy-done.81), channel_id=1, source_target_pairs={{0,5},{1,4},{2,7},{3,6},{4,1},{5,0},{6,3},{7,2},{8,13},{9,12},{10,... | collective-permute-start | bytes 786440 | tf_op jit(solution)/shard_map/ppermute | solution.py:450
  145.5 48.0 %collective-permute-start.22 = (f32[17,2,32,128]{3,2,1,0:T(8,128)}, f32[17,2,32,128]{3,2,1,0:T(8,128)S(1)}, u32[]{:S(2)}, u32[]{:S(2)}) collective-permute-start(f32[17,2,32,128]{3,2,1,0:T(8,128)} %get-tuple-element.134), channel_id=1, source_target_pairs={{0,8},{8,0},{16,24},{24,16},{1,9},{9,1},{17,25},{25,17},{2,10},{10... | collective-permute-start | bytes 1671176 | tf_op jit(solution)/shard_map/ppermute | solution.py:450
  150.7 43.6 %collective-permute-start.23 = (f32[17,2,32,128]{3,2,1,0:T(8,128)}, f32[17,2,32,128]{3,2,1,0:T(8,128)S(1)}, u32[]{:S(2)}, u32[]{:S(2)}) collective-permute-start(f32[17,2,32,128]{3,2,1,0:T(8,128)} %get-tuple-element.135), channel_id=1, source_target_pairs={{0,16},{8,24},{16,0},{24,8},{1,17},{9,25},{17,1},{25,9},{2,18},{10... | collective-permute-start | bytes 1671176 | tf_op jit(solution)/shard_map/ppermute | solution.py:450
  152.9 43.4 %collective-permute-start.24 = (f32[17,2,32,128]{3,2,1,0:T(8,128)}, f32[17,2,32,128]{3,2,1,0:T(8,128)S(1)}, u32[]{:S(2)}, u32[]{:S(2)}) collective-permute-start(f32[17,2,32,128]{3,2,1,0:T(8,128)} %get-tuple-element.136), channel_id=1, source_target_pairs={{0,24},{8,16},{16,8},{24,0},{1,25},{9,17},{17,9},{25,1},{2,26},{10... | collective-permute-start | bytes 1671176 | tf_op jit(solution)/shard_map/ppermute | solution.py:450
  154.6 35.0 %collective-permute-start.16 = (f32[8,2,32,128]{3,2,1,0:T(8,128)}, f32[8,2,32,128]{3,2,1,0:T(8,128)S(1)}, u32[]{:S(2)}, u32[]{:S(2)}) collective-permute-start(f32[8,2,32,128]{3,2,1,0:T(8,128)} %get-tuple-element.126), channel_id=1, source_target_pairs={{0,3},{1,2},{2,1},{3,0},{4,7},{5,6},{6,5},{7,4},{8,11},{9,10},{10,... | collective-permute-start | bytes 786440 | tf_op jit(solution)/shard_map/ppermute | solution.py:450
  234.8 34.7 %collective-permute-start.31 = (f32[8,2,32,128]{3,2,1,0:T(8,128)}, f32[8,2,32,128]{3,2,1,0:T(8,128)}, u32[]{:S(2)}, u32[]{:S(2)}) collective-permute-start(f32[8,2,32,128]{3,2,1,0:T(8,128)} %get-tuple-element.144), channel_id=1, source_target_pairs={{0,7},{1,6},{2,5},{3,4},{4,3},{5,2},{6,1},{7,0},{8,15},{9,14},{10,... | collective-permute-start | bytes 786440 | tf_op jit(solution)/shard_map/ppermute | solution.py:450
  241.6 38.5 %collective-permute-start.36 = (f32[8,2,32,128]{3,2,1,0:T(8,128)}, f32[8,2,32,128]{3,2,1,0:T(8,128)}, u32[]{:S(2)}, u32[]{:S(2)}) collective-permute-start(f32[8,2,32,128]{3,2,1,0:T(8,128)} %get-tuple-element.152), channel_id=1, source_target_pairs={{0,1},{1,0},{2,3},{3,2},{4,5},{5,4},{6,7},{7,6},{8,9},{9,8},{10,11... | collective-permute-start | bytes 786440 | tf_op jit(solution)/shard_map/ppermute | solution.py:450
  242.1 40.4 %collective-permute-start.37 = (f32[8,2,32,128]{3,2,1,0:T(8,128)}, f32[8,2,32,128]{3,2,1,0:T(8,128)}, u32[]{:S(2)}, u32[]{:S(2)}) collective-permute-start(f32[8,2,32,128]{3,2,1,0:T(8,128)} %get-tuple-element.153), channel_id=1, source_target_pairs={{0,2},{1,3},{2,0},{3,1},{4,6},{5,7},{6,4},{7,5},{8,10},{9,11},{10,... | collective-permute-start | bytes 786440 | tf_op jit(solution)/shard_map/ppermute | solution.py:450
  262.8 39.8 %collective-permute-start.39 = (f32[8,2,32,128]{3,2,1,0:T(8,128)}, f32[8,2,32,128]{3,2,1,0:T(8,128)}, u32[]{:S(2)}, u32[]{:S(2)}) collective-permute-start(f32[8,2,32,128]{3,2,1,0:T(8,128)} %get-tuple-element.155), channel_id=1, source_target_pairs={{0,4},{1,5},{2,6},{3,7},{4,0},{5,1},{6,2},{7,3},{8,12},{9,13},{10,... | collective-permute-start | bytes 786440 | tf_op jit(solution)/shard_map/ppermute | solution.py:450
  269.4 38.3 %collective-permute-start.40 = (f32[8,2,32,128]{3,2,1,0:T(8,128)}, f32[8,2,32,128]{3,2,1,0:T(8,128)}, u32[]{:S(2)}, u32[]{:S(2)}) collective-permute-start(f32[8,2,32,128]{3,2,1,0:T(8,128)} %get-tuple-element.156), channel_id=1, source_target_pairs={{0,5},{1,4},{2,7},{3,6},{4,1},{5,0},{6,3},{7,2},{8,13},{9,12},{10,... | collective-permute-start | bytes 786440 | tf_op jit(solution)/shard_map/ppermute | solution.py:450
  331.7 35.2 %collective-permute-start.47 = (f32[8,8,8,128]{3,2,1,0:T(8,128)}, f32[8,8,8,128]{3,2,1,0:T(8,128)S(1)}, u32[]{:S(2)}, u32[]{:S(2)}) collective-permute-start(f32[8,8,8,128]{3,2,1,0:T(8,128)} %get-tuple-element.164), channel_id=1, source_target_pairs={{0,5},{1,4},{2,7},{3,6},{4,1},{5,0},{6,3},{7,2},{8,13},{9,12},{10,... | collective-permute-start | bytes 786440 | tf_op jit(solution)/shard_map/ppermute | solution.py:450
  342.5 34.5 %collective-permute-start.48 = (f32[8,8,8,128]{3,2,1,0:T(8,128)S(1)}, f32[8,8,8,128]{3,2,1,0:T(8,128)S(1)}, u32[]{:S(2)}, u32[]{:S(2)}) collective-permute-start(f32[8,8,8,128]{3,2,1,0:T(8,128)S(1)} %copy-done.89), channel_id=1, source_target_pairs={{0,6},{1,7},{2,4},{3,5},{4,2},{5,3},{6,0},{7,1},{8,14},{9,15},{10,... | collective-permute-start | bytes 786440 | tf_op jit(solution)/shard_map/ppermute | solution.py:450
  380.0 35.6 %collective-permute-start.57 = (f32[8,8,8,128]{3,2,1,0:T(8,128)S(1)}, f32[8,8,8,128]{3,2,1,0:T(8,128)S(1)}, u32[]{:S(2)}, u32[]{:S(2)}) collective-permute-start(f32[8,8,8,128]{3,2,1,0:T(8,128)S(1)} %copy-done.68), channel_id=1, source_target_pairs={{0,5},{1,4},{2,7},{3,6},{4,1},{5,0},{6,3},{7,2},{8,13},{9,12},{10,... | collective-permute-start | bytes 786440 | tf_op jit(solution)/shard_map/ppermute | solution.py:450
  380.8 34.8 %collective-permute-start.58 = (f32[8,8,8,128]{3,2,1,0:T(8,128)S(1)}, f32[8,8,8,128]{3,2,1,0:T(8,128)S(1)}, u32[]{:S(2)}, u32[]{:S(2)}) collective-permute-start(f32[8,8,8,128]{3,2,1,0:T(8,128)S(1)} %copy-done.64), channel_id=1, source_target_pairs={{0,6},{1,7},{2,4},{3,5},{4,2},{5,3},{6,0},{7,1},{8,14},{9,15},{10,... | collective-permute-start | bytes 786440 | tf_op jit(solution)/shard_map/ppermute | solution.py:450
  382.6 39.8 %collective-permute-start.59 = (f32[8,8,8,128]{3,2,1,0:T(8,128)S(1)}, f32[8,8,8,128]{3,2,1,0:T(8,128)S(1)}, u32[]{:S(2)}, u32[]{:S(2)}) collective-permute-start(f32[8,8,8,128]{3,2,1,0:T(8,128)S(1)} %copy-done.60), channel_id=1, source_target_pairs={{0,7},{1,6},{2,5},{3,4},{4,3},{5,2},{6,1},{7,0},{8,15},{9,14},{10,... | collective-permute-start | bytes 786440 | tf_op jit(solution)/shard_map/ppermute | solution.py:450
  383.5 49.5 %collective-permute-start.63 = (f32[8,8,8,128]{3,2,1,0:T(8,128)}, f32[8,8,8,128]{3,2,1,0:T(8,128)S(1)}, u32[]{:S(2)}, u32[]{:S(2)}) collective-permute-start(f32[8,8,8,128]{3,2,1,0:T(8,128)} %get-tuple-element.184), channel_id=1, source_target_pairs={{0,1},{1,0},{2,3},{3,2},{4,5},{5,4},{6,7},{7,6},{8,9},{9,8},{10,11... | collective-permute-start | bytes 786440 | tf_op jit(solution)/shard_map/ppermute | solution.py:450
  415.6 38.6 %collective-permute-start.66 = (f32[8,8,8,128]{3,2,1,0:T(8,128)S(1)}, f32[8,8,8,128]{3,2,1,0:T(8,128)S(1)}, u32[]{:S(2)}, u32[]{:S(2)}) collective-permute-start(f32[8,8,8,128]{3,2,1,0:T(8,128)S(1)} %copy-done.61), channel_id=1, source_target_pairs={{0,4},{1,5},{2,6},{3,7},{4,0},{5,1},{6,2},{7,3},{8,12},{9,13},{10,... | collective-permute-start | bytes 786440 | tf_op jit(solution)/shard_map/ppermute | solution.py:450
  422.4 38.2 %collective-permute-start.67 = (f32[8,8,8,128]{3,2,1,0:T(8,128)S(1)}, f32[8,8,8,128]{3,2,1,0:T(8,128)S(1)}, u32[]{:S(2)}, u32[]{:S(2)}) collective-permute-start(f32[8,8,8,128]{3,2,1,0:T(8,128)S(1)} %copy-done.58), channel_id=1, source_target_pairs={{0,5},{1,4},{2,7},{3,6},{4,1},{5,0},{6,3},{7,2},{8,13},{9,12},{10,... | collective-permute-start | bytes 786440 | tf_op jit(solution)/shard_map/ppermute | solution.py:450
  442.6 35.4 %collective-permute-start.73 = (f32[8,8,8,128]{3,2,1,0:T(8,128)}, f32[8,8,8,128]{3,2,1,0:T(8,128)S(1)}, u32[]{:S(2)}, u32[]{:S(2)}) collective-permute-start(f32[8,8,8,128]{3,2,1,0:T(8,128)} %get-tuple-element.196), channel_id=1, source_target_pairs={{0,1},{1,0},{2,3},{3,2},{4,5},{5,4},{6,7},{7,6},{8,9},{9,8},{10,11... | collective-permute-start | bytes 786440 | tf_op jit(solution)/shard_map/ppermute | solution.py:450
  460.6 38.6 %collective-permute-start.76 = (f32[8,8,8,128]{3,2,1,0:T(8,128)}, f32[8,8,8,128]{3,2,1,0:T(8,128)S(1)}, u32[]{:S(2)}, u32[]{:S(2)}) collective-permute-start(f32[8,8,8,128]{3,2,1,0:T(8,128)} %get-tuple-element.199), channel_id=1, source_target_pairs={{0,4},{1,5},{2,6},{3,7},{4,0},{5,1},{6,2},{7,3},{8,12},{9,13},{10,... | collective-permute-start | bytes 786440 | tf_op jit(solution)/shard_map/ppermute | solution.py:450
  474.1 34.1 %collective-permute-start.77 = (f32[8,8,8,128]{3,2,1,0:T(8,128)S(1)}, f32[8,8,8,128]{3,2,1,0:T(8,128)S(1)}, u32[]{:S(2)}, u32[]{:S(2)}) collective-permute-start(f32[8,8,8,128]{3,2,1,0:T(8,128)S(1)} %copy-done.45), channel_id=1, source_target_pairs={{0,5},{1,4},{2,7},{3,6},{4,1},{5,0},{6,3},{7,2},{8,13},{9,12},{10,... | collective-permute-start | bytes 786440 | tf_op jit(solution)/shard_map/ppermute | solution.py:450
  509.8 38.3 %collective-permute-start.61 = (f32[16,8,8,128]{3,2,1,0:T(8,128)}, f32[16,8,8,128]{3,2,1,0:T(8,128)S(1)}, u32[]{:S(2)}, u32[]{:S(2)}) collective-permute-start(f32[16,8,8,128]{3,2,1,0:T(8,128)} %get-tuple-element.181), channel_id=1, source_target_pairs={{0,16},{8,24},{16,0},{24,8},{1,17},{9,25},{17,1},{25,9},{2,18},{10... | collective-permute-start | bytes 1572872 | tf_op jit(solution)/shard_map/ppermute | solution.py:450
  511.7 37.2 %collective-permute-start.62 = (f32[16,8,8,128]{3,2,1,0:T(8,128)}, f32[16,8,8,128]{3,2,1,0:T(8,128)S(1)}, u32[]{:S(2)}, u32[]{:S(2)}) collective-permute-start(f32[16,8,8,128]{3,2,1,0:T(8,128)} %get-tuple-element.182), channel_id=1, source_target_pairs={{0,24},{8,16},{16,8},{24,0},{1,25},{9,17},{17,9},{25,1},{2,26},{10... | collective-permute-start | bytes 1572872 | tf_op jit(solution)/shard_map/ppermute | solution.py:450
  533.1 37.5 %collective-permute-start.71 = (f32[16,8,8,128]{3,2,1,0:T(8,128)}, f32[16,8,8,128]{3,2,1,0:T(8,128)}, u32[]{:S(2)}, u32[]{:S(2)}) collective-permute-start(f32[16,8,8,128]{3,2,1,0:T(8,128)} %get-tuple-element.193), channel_id=1, source_target_pairs={{0,16},{8,24},{16,0},{24,8},{1,17},{9,25},{17,1},{25,9},{2,18},{10... | collective-permute-start | bytes 1572872 | tf_op jit(solution)/shard_map/ppermute | solution.py:450
  535.1 35.5 %collective-permute-start.72 = (f32[16,8,8,128]{3,2,1,0:T(8,128)}, f32[16,8,8,128]{3,2,1,0:T(8,128)}, u32[]{:S(2)}, u32[]{:S(2)}) collective-permute-start(f32[16,8,8,128]{3,2,1,0:T(8,128)} %get-tuple-element.194), channel_id=1, source_target_pairs={{0,24},{8,16},{16,8},{24,0},{1,25},{9,17},{17,9},{25,1},{2,26},{10... | collective-permute-start | bytes 1572872 | tf_op jit(solution)/shard_map/ppermute | solution.py:450
  548.9 44.0 %collective-permute-start.81 = (f32[16,8,8,128]{3,2,1,0:T(8,128)}, f32[16,8,8,128]{3,2,1,0:T(8,128)}, u32[]{:S(2)}, u32[]{:S(2)}) collective-permute-start(f32[16,8,8,128]{3,2,1,0:T(8,128)} %get-tuple-element.205), channel_id=1, source_target_pairs={{0,16},{8,24},{16,0},{24,8},{1,17},{9,25},{17,1},{25,9},{2,18},{10... | collective-permute-start | bytes 1572872 | tf_op jit(solution)/shard_map/ppermute | solution.py:450
  557.0 35.9 %collective-permute-start.82 = (f32[16,8,8,128]{3,2,1,0:T(8,128)}, f32[16,8,8,128]{3,2,1,0:T(8,128)}, u32[]{:S(2)}, u32[]{:S(2)}) collective-permute-start(f32[16,8,8,128]{3,2,1,0:T(8,128)} %get-tuple-element.206), channel_id=1, source_target_pairs={{0,24},{8,16},{16,8},{24,0},{1,25},{9,17},{17,9},{25,1},{2,26},{10... | collective-permute-start | bytes 1572872 | tf_op jit(solution)/shard_map/ppermute | solution.py:450
  (143 other events, 6181.2 us)

commit v2 on v1

--- a/solution.py
+++ b/solution.py
@@ -198,7 +198,7 @@
 
 
 def cost(cells, picoseconds):
-    return pl.CostEstimate(flops=int(cells * picoseconds * 1150), bytes_accessed=0, transcendentals=0)
+    return pl.CostEstimate(flops=int(cells * picoseconds * 500), bytes_accessed=0, transcendentals=0)
 
 
 def params():
@@ -208,7 +208,7 @@
 def pointwise(first_row, lead, count, n_tm, operands, tables, fx_in, nm):
     potential, multiplier = operands[1], operands[2]
     steps, rows, width, _ = potential.shape
-    flags, potential, multiplier, start, final, ahead_t, ahead_x = operands
+    flags, potential, multiplier, start, final, (from_row, ahead_t), ahead_x = operands
     here = lambda i: jnp.minimum(first_row - lead + i, rows - 1)
     slot = lambda i: jnp.maximum(i - lead, 0)
     plane = (width, LANES)
@@ -217,7 +217,7 @@
         pl.BlockSpec(memory_space=pltpu.SMEM),
         pl.BlockSpec((steps, 1) + plane, lambda i: (0, here(i), 0, 0)),
         pl.BlockSpec((steps, 1) + plane, lambda i: (0, here(i + 1), 0, 0)),
-        pl.BlockSpec((1, 1) + plane, lambda i: (0, here(i), 0, 0)),
+        pl.BlockSpec((1, 1) + plane, lambda i: (0, here(i) - from_row, 0, 0)),
         pl.BlockSpec((4, steps, 1) + plane, lambda i: (0, 0, here(i), 0, 0)),
         pl.BlockSpec((1,) + plane, lambda i: (here(i), 0, 0)),
         pl.BlockSpec((1,) + plane, lambda i: (here(i), 0, 0)),
@@ -266,10 +266,9 @@
 
 
 def time_kernel(steps, n_sp, spot, *refs):
-    t_all, stage = refs[-2:]
-    got, out = refs[: -2 - n_sp], refs[-2 - n_sp : -2]
+    got, (out, t_all) = refs[:-2], refs[-2:]
     n = len(got)
-    me_t, me_x = spot[0, 0], spot[0, 1]
+    me_t = spot[0, 0]
     total = n * steps
     share = total // n_sp
 
@@ -284,9 +283,7 @@
             xs[(b + 1) * steps - 1] = xs[(b + 1) * steps - 1] + flux
             xs[(b + 1) * steps] = xs[(b + 1) * steps] - flux
         for k, v in enumerate(dct(xs)):
-            stage[(k // share) ^ me_x, k % share] = v
-        for d in range(n_sp):
-            out[d][:, 0, at, :] = stage[d]
+            out[k // share, k % share, 0, at, :] = v
         return carry
 
     lax.fori_loop(0, got[0].shape[2] // GROUP, group, 0)
@@ -301,75 +298,61 @@
         grid=(count,),
         in_specs=[pl.BlockSpec(memory_space=pltpu.SMEM)]
         + [pl.BlockSpec((planes, 1, block, lanes), lambda i: (0, i, 0, 0))] * n,
-        out_specs=[pl.BlockSpec((share, 1, block, lanes), lambda i: (0, i, 0, 0))] * n_sp,
-        out_shape=[jax.ShapeDtypeStruct((share, count, block, lanes), jnp.float32)] * n_sp,
-        scratch_shapes=[
-            pltpu.VMEM((n, planes, GROUP, lanes), jnp.float32),
-            pltpu.VMEM((n_sp, share, GROUP, lanes), jnp.float32),
-        ],
+        out_specs=pl.BlockSpec((n_sp, share, 1, block, lanes), lambda i: (0, 0, i, 0, 0)),
+        out_shape=jax.ShapeDtypeStruct((n_sp, share, count, block, lanes), jnp.float32),
+        scratch_shapes=[pltpu.VMEM((n, planes, GROUP, lanes), jnp.float32)],
         compiler_params=params(),
         cost_estimate=cost(got[0].size * n, 10),
         name="time",
     )(spot, *got)
 
 
-def middle_kernel(n_sp, first_rows, spot, sig, *refs):
-    x_all, stage = refs[-2:]
-    got, out = refs[: -2 - n_sp], refs[-2 - n_sp : -2]
-    me = spot[0, 1]
-    share, count = got[0].shape[:2]
-    rows = count * len(first_rows)
+def middle_kernel(n_sp, first_rows, sig, *refs):
+    got, outs = refs[: len(first_rows)], refs[len(first_rows) :]
+    share = got[0].shape[1]
+    rows = sum(part.shape[2] for part in got)
+    each = rows // len(outs)
     eig = RATE * eigen(rows * n_sp)
+    parts = sorted(zip(first_rows, got), key=lambda part: part[0])
 
     def one(k, carry):
-        for c, first in enumerate(first_rows):
-            for d in range(n_sp):
-                for r in range(count):
-                    x_all[d ^ me, first + r] = got[c * n_sp + d][k, r]
-        xs = dct([x_all[j, r] for j in range(n_sp) for r in range(rows)])
+        xs = dct([part[j, k, r] for j in range(n_sp) for _, part in parts for r in range(part.shape[2])])
         base = sig[k]
         xs = [x * refined(base + float(eig[i])) for i, x in enumerate(xs)]
         for x, v in enumerate(dct(xs)):
-            stage[(x // rows) ^ me, x % rows] = v
-        for d in range(n_sp):
-            out[d][k] = stage[d]
+            r = x % rows
+            outs[r // each][x // rows, k, r % each] = v
         return carry
 
     lax.fori_loop(0, share, one, 0)
 
 
-def middle(g, spot, sig, got, first_rows, n_sp):
-    share, count, block, lanes = got[0].shape
-    rows = count * len(first_rows)
-    f32 = jnp.float32
-    size = n_sp * share * rows * GROUP * lanes
+def middle(g, sig, got, first_rows, pieces):
+    n_sp, share, _, block, lanes = got[0].shape
+    rows = sum(part.shape[2] for part in got)
+    out = (n_sp, share, rows // pieces, GROUP, lanes)
     return pl.pallas_call(
         lambda *refs: middle_kernel(n_sp, first_rows, *refs),
         grid=(1,),
-        in_specs=[
-            pl.BlockSpec(memory_space=pltpu.SMEM),
-            pl.BlockSpec((share, GROUP, lanes), lambda i: (0, g, 0)),
-        ]
-        + [pl.BlockSpec((share, count, GROUP, lanes), lambda i: (0, 0, g, 0))] * len(got),
-        out_specs=[pl.BlockSpec((share, rows, GROUP, lanes), lambda i: (0, 0, 0, 0))] * n_sp,
-        out_shape=[jax.ShapeDtypeStruct((share, rows, GROUP, lanes), f32)] * n_sp,
-        scratch_shapes=[pltpu.VMEM((n_sp, rows, GROUP, lanes), f32)] * 2,
+        in_specs=[pl.BlockSpec((share, GROUP, lanes), lambda i: (0, g, 0))]
+        + [
+            pl.BlockSpec(part.shape[:3] + (GROUP, lanes), lambda i: (0, 0, 0, g, 0)) for part in got
+        ],
+        out_specs=[pl.BlockSpec(out, lambda i: (0, 0, 0, 0, 0))] * pieces,
+        out_shape=[jax.ShapeDtypeStruct(out, jnp.float32)] * pieces,
         compiler_params=params(),
-        cost_estimate=cost(size, 18),
+        cost_estimate=cost(math.prod(out) * pieces, 18),
         name="middle",
-    )(spot, sig, *got)
-
-
-def untime_kernel(steps, n_tm, spot, *refs):
-    k_all, stage = refs[-2:]
-    got, out = refs[: -2 - n_tm], refs[-2 - n_tm : -2]
-    me_t, me_x = spot[0, 0], spot[0, 1]
-    share, rows = got[0].shape[:2]
+    )(sig, *got)
+
+
+def untime_kernel(steps, n_tm, spot, got, *refs):
+    out, stage = refs[:-1], refs[-1]
+    me_t = spot[0, 0]
+    n, share, rows = got.shape[:3]
 
     def one(r, carry):
-        for d in range(len(got)):
-            k_all[d ^ me_x] = got[d][:, r]
-        xs = dct([k_all[j, k] for j in range(len(got)) for k in range(share)])
+        xs = dct([got[j, k, r] for j in range(n) for k in range(share)])
         for t, v in enumerate(xs):
             stage[(t // steps) ^ me_t, t % steps] = v
         for d in range(n_tm):
@@ -380,34 +363,32 @@
 
 
 def untime(spot, got, n_tm):
-    share, rows, group, lanes = got[0].shape
-    steps = share * len(got) // n_tm
+    n_sp, share, rows, group, lanes = got.shape
+    steps = share * n_sp // n_tm
     f32 = jnp.float32
-    size = n_tm * steps * rows * group * lanes
     return pl.pallas_call(
         lambda *refs: untime_kernel(steps, n_tm, *refs),
         grid=(1,),
-        in_specs=[pl.BlockSpec(memory_space=pltpu.SMEM)]
-        + [pl.BlockSpec(got[0].shape, lambda i: (0, 0, 0, 0))] * len(got),
+        in_specs=[
+            pl.BlockSpec(memory_space=pltpu.SMEM),
+            pl.BlockSpec(got.shape, lambda i: (0, 0, 0, 0, 0)),
+        ],
         out_specs=[pl.BlockSpec((steps, rows, group, lanes), lambda i: (0, 0, 0, 0))] * n_tm,
         out_shape=[jax.ShapeDtypeStruct((steps, rows, group, lanes), f32)] * n_tm,
-        scratch_shapes=[
-            pltpu.VMEM((len(got), share, group, lanes), f32),
-            pltpu.VMEM((n_tm, steps, group, lanes), f32),
-        ],
+        scratch_shapes=[pltpu.VMEM((n_tm, steps, group, lanes), f32)],
         compiler_params=params(),
-        cost_estimate=cost(size, 11),
+        cost_estimate=cost(got.size, 11),
         name="untime",
-    )(spot, *got)
-
-
-def back_kernel(*refs):
-    got, (cy, cz, out, whole) = refs[:-4], refs[-4:]
+    )(spot, got)
+
+
+def back_kernel(n_got, *refs):
+    got, cy, cz = refs[:n_got], refs[n_got], refs[n_got + 1]
+    out, whole = refs[-2:]
+    batch = min(BATCH, out.shape[0])
     for t in range(out.shape[0]):
         for n, part in enumerate(got):
             whole[t, pl.ds(n * GROUP, GROUP), :] = part[t, 0]
-
-    batch = min(BATCH, out.shape[0])
 
     def some(b, carry):
         planes = [whole[b * batch + k] for k in range(batch)]
@@ -418,24 +399,33 @@
     lax.fori_loop(0, out.shape[0] // batch, some, 0)
 
 
-def back(got, cy, cz):
-    steps, rows, group, lanes = got[0].shape
+def back(first, count, rows, got, cy, cz, result):
+    steps, _, group, lanes = got[0][1].shape
     width = group * len(got)
+    in_specs = [
+        pl.BlockSpec((steps, 1, group, lanes), lambda i, skip=first - at: (0, i + skip, 0, 0)) for at, _ in got
+    ] + [
+        pl.BlockSpec((width, 3 * width), lambda i: (0, 0)),
+        pl.BlockSpec((3 * lanes, lanes), lambda i: (0, 0)),
+    ]
+    inputs = [part for _, part in got] + [cy, cz]
+    aliases = {}
+    if result is not None:
+        in_specs.append(pl.BlockSpec(memory_space=pl.ANY))
+        aliases = {len(inputs): 0}
+        inputs.append(result)
     return pl.pallas_call(
-        back_kernel,
-        grid=(rows,),
-        in_specs=[pl.BlockSpec((steps, 1, group, lanes), lambda i: (0, i, 0, 0))] * len(got)
-        + [
-            pl.BlockSpec((width, 3 * width), lambda i: (0, 0)),
-            pl.BlockSpec((3 * lanes, lanes), lambda i: (0, 0)),
-        ],
-        out_specs=pl.BlockSpec((steps, 1, width, lanes), lambda i: (0, i, 0, 0)),
+        lambda *refs: back_kernel(len(got), *refs),
+        grid=(count,),
+        in_specs=in_specs,
+        out_specs=pl.BlockSpec((steps, 1, width, lanes), lambda i: (0, first + i, 0, 0)),
         out_shape=jax.ShapeDtypeStruct((steps, rows, width, lanes), jnp.float32),
         scratch_shapes=[pltpu.VMEM((steps, width, lanes), jnp.float32)],
+        input_output_aliases=aliases,
         compiler_params=params(),
-        cost_estimate=cost(steps * rows * width * lanes, 7),
+        cost_estimate=cost(steps * count * width * lanes, 7),
         name="back",
-    )(*got, cy, cz)
+    )(*inputs)
 
 
 def from_behind(block, axis, distance):
@@ -449,6 +439,10 @@
     return [parts[0]] + [
         lax.ppermute(parts[d], axis, [(i, i ^ d) for i in devices]) for d in range(1, len(parts))
     ]
+
+
+def swap(parts):
+    return lax.all_to_all(parts, "space", split_axis=0, concat_axis=0, tiled=True)
 
 
 def body(potential, multiplier, start_density, final_density):
@@ -461,10 +455,15 @@
     block = width // n_tm
     groups = block // GROUP
     share = total_t // n_sp
-    parts = min(rows, 4)
-    count = rows // parts
+    size = 2 if rows > 4 and rows % 2 == 0 else 1
+    inner = [1 + size * n for n in range((rows - 2) // size)]
+    firsts = [1, rows - 1] + inner[1:] + [0]
+    counts = [size, 1] + [size] * (len(inner) - 1) + [1]
+    leads = [1, 1] + [0] * (len(counts) - 2)
     f32 = jnp.float32
-    ahead_t = from_behind(potential[:1], "tm", -1)
+    early = size + 1
+    ahead_t = (0, from_behind(potential[:1, :early], "tm", -1))
+    ahead_rest = (early, from_behind(potential[:1, early:], "tm", -1))
     ahead_x = from_behind(potential[:, :1], "space", -1)
     flags = jnp.stack(
         [me_t < n_tm - 1, me_x < n_sp - 1, me_t == 0, me_t == n_tm - 1]
@@ -486,26 +485,66 @@
     eig_yz = lax.dynamic_slice_in_dim(eig_yz, me_t * block, block, 0)[None]
     sig = RATE * (eig_t + eig_yz) + PROX
 
-    operands = (flags, potential, multiplier, start_density, final_density, ahead_t, ahead_x)
     flux, next_multiplier = None, None
-    moved, first_rows = [], []
-    for n in range(parts):
-        first = ((n + 1) % parts) * count
-        if first == 0:
-            flux = from_behind(flux, "space", 1)
-        next_multiplier, flux, *pay = pointwise(
-            first, 1 if n == 0 else 0, count, n_tm, operands, tables, flux, next_multiplier
+    ready, moved, waiting, behind = [], [], None, None
+    for n, (first, count, lead) in enumerate(zip(firsts, counts, leads)):
+        operands = (
+            flags, potential, multiplier, start_density, final_density,
+            ahead_t if first < early else ahead_rest, ahead_x,
         )
-        timed = time_transform(spot, trade(pay, "tm"), n_sp)
-        moved += trade(timed, "space")
-        first_rows.append(first)
-    final = []
+        next_multiplier, new_flux, *pay = pointwise(
+            first, lead, count, n_tm, operands, tables, flux if first else behind, next_multiplier
+        )
+        if first == rows - 1:
+            behind = new_flux
+        else:
+            flux = new_flux
+        if n == 2:
+            behind, _, _ = lax.optimization_barrier((behind, moved[0], pay[0]))
+            behind = from_behind(behind, "space", 1)
+        if n:
+            waiting, next_multiplier = lax.optimization_barrier((waiting, next_multiplier))
+            ready.append(time_transform(spot, waiting, n_sp))
+            _, next_multiplier = lax.optimization_barrier((ready[-1], next_multiplier))
+        if n == 1:
+            moved.append(swap(ready[0]))
+        waiting = trade(pay, "tm")
+    ready.append(time_transform(spot, waiting, n_sp))
+
+    for n, timed in enumerate(ready):
+        if n == 0:
+            continue
+        if n == 1:
+            timed, _ = lax.optimization_barrier((timed, behind))
+        if n == len(ready) - 2:
+            timed, _ = lax.optimization_barrier((timed, ready[-1]))
+        timed, _ = lax.optimization_barrier((timed, moved[-1]))
+        moved.append(swap(timed))
+
+    pieces = 2 if rows % 2 == 0 else 1
+    solved = []
     for g in range(groups):
-        solved = middle(g, spot, sig, moved, first_rows, n_sp)
-        solved = trade(solved, "space")
-        steps_of = untime(spot, solved, n_tm)
-        final += trade(steps_of, "tm")
-    next_potential = back(final, columns_y, cos_z)
+        solved += middle(g, sig, moved, firsts, pieces if g == groups - 1 else 1)
+    final, done, back_x = [], [], []
+    for n, part in enumerate(solved):
+        if n:
+            part, _ = lax.optimization_barrier((part, back_x[-1]))
+        if n + 1 < len(solved) and n >= 2:
+            part, final[n - 2] = lax.optimization_barrier((part, final[n - 2]))
+        elif n >= 2:
+            part, _ = lax.optimization_barrier((part, done[n - 2]))
+        part = swap(part)
+        back_x.append(part)
+        if n + 1 == len(solved) and n >= 2:
+            part, final[n - 2] = lax.optimization_barrier((part, final[n - 2]))
+        done.append(untime(spot, part, n_tm))
+        final.append(trade(done[-1], "tm"))
+    next_potential = None
+    size = rows // pieces
+    for piece in range(pieces):
+        got = [(0, part) for some in final[: groups - 1] for part in some]
+        got += [(piece * size, part) for part in final[groups - 1 + piece]]
+        next_potential = back(piece * size, size, rows, got, columns_y, cos_z, next_potential)
     return (next_potential, next_multiplier)
 
 

time: 615 us -> 606 us (0.985)
  starting transfers between devices: 176 us -> 82.1 us
  blocking collectives: 0 us -> 53.4 us
  Pallas kernels: 192 us -> 207 us
  local copies, waits for them, and re-layouts: 10.9 us -> 20.1 us
  waiting for transfers between devices: 224 us -> 232 us
    all_to_all x0 -> x9, waiting for transfers between devices: none -> 176 us  [swap(): lax.all_to_all(parts, 'space', split_axis=0, concat_axis=0, tiled=True)]
    ppermute x80 -> x30, waiting for transfers between devices: 215 us -> 54.9 us  [trade(): lax.ppermute(parts[d], axis, [(i, i ^ d) for i in devices])]
    ppermute x80 -> x30, starting transfers between devices: 171 us -> 38.8 us  [trade(): lax.ppermute(parts[d], axis, [(i, i ^ d) for i in devices])]
    all_to_all x0 -> x1, blocking collectives: none -> 53.4 us  [swap(): lax.all_to_all(parts, 'space', split_axis=0, concat_axis=0, tiled=True)]
    all_to_all x0 -> x9, starting transfers between devices: none -> 37.8 us  [swap(): lax.all_to_all(parts, 'space', split_axis=0, concat_axis=0, tiled=True)]
    pallas_call x4 -> x5, Pallas kernels: 86.6 us -> 98.6 us  [pointwise(): pl.pallas_call(lambda *refs: pointwise_kernel(len(inputs), first_row, lea...]
    unnamed x184 -> x96, local copies, waits for them, and re-layouts: 3.95 us -> 13.1 us
    ppermute x3 -> x4, waiting for transfers between devices: 9.27 us -> 1.59 us  [from_behind(): return lax.ppermute(block, axis, route)]
  transfers between devices with their start and end apart: 83 -> 43, of which waited for: 26 -> 24; matrix products, arithmetic and copies ran while one was open for 1% -> 1% of each run, Pallas kernels for 28% -> 31%
where the time goes in v2:
time: 606 us; the launch traced here: 598 us
  waiting for transfers between devices  232 us (38%)
  Pallas kernels  207 us (34%)
  starting transfers between devices  82.1 us (14%)
  blocking collectives  53.4 us (9%)
  local copies, waits for them, and re-layouts  20.1 us (3%)
    all_to_all x9, waiting for transfers between devices, swap(): lax.all_to_all(parts, 'space', split_axis=0, concat_axis=0, tiled=True)  176 us
    pallas_call x5, Pallas kernels, pointwise(): pl.pallas_call(lambda *refs: pointwise_kernel(len(inputs), first_row, lea...  98.6 us
    ppermute x30, waiting for transfers between devices, trade(): lax.ppermute(parts[d], axis, [(i, i ^ d) for i in devices])  54.9 us
    all_to_all x1, blocking collectives, swap(): lax.all_to_all(parts, 'space', split_axis=0, concat_axis=0, tiled=True)  53.4 us
    ppermute x30, starting transfers between devices, trade(): lax.ppermute(parts[d], axis, [(i, i ^ d) for i in devices])  38.8 us
    pallas_call x4, Pallas kernels, middle(): pl.pallas_call(lambda *refs: middle_kernel(n_sp, first_rows, *refs), grid...  38.6 us
    all_to_all x9, starting transfers between devices, swap(): lax.all_to_all(parts, 'space', split_axis=0, concat_axis=0, tiled=True)  37.8 us
    pallas_call x5, Pallas kernels, untime(): pl.pallas_call(lambda *refs: untime_kernel(steps, n_tm, *refs), grid=(1,)...  28 us
  transfers between devices with their start and end apart: 43, of which 24 were waited for; matrix products, arithmetic and copies ran while one was open for 1% of the time, Pallas kernels for 31%

profile of v2, /device:TPU:0, one launch (start us, length us, event | category | flops | bytes accessed | tf_op | source)
XLA Modules:
  0.0 598.0 jit_solution(12642828061381788919)
XLA Ops:
  12.9 26.3 %pointwise.5 = (f32[4,16,8,128,128]{4,3,2,1,0:T(8,128)}, f32[16,128,128]{2,1,0:T(8,128)}, f32[17,2,32,128]{3,2,1,0:T(8,128)}, f32[17,2,32,128]{3,2,1,0:T(8,128)}...) custom-call(f32[1,4]{1,0:T(1,128)} %add_convert_fusion.refs_0_, f32[16,8,128,128]{3,2,1,0:T(8,128)} %refs_2_.9, ...), custom_call_target="tpu_custom_call" | custom-call | flops 14155776000 | tf_op jit(solution)/shard_map/pointwise/pallas_call | solution.py:241
  46.4 20.1 %pointwise.6 = (f32[4,16,8,128,128]{4,3,2,1,0:T(8,128)}, f32[16,128,128]{2,1,0:T(8,128)}, f32[17,1,32,128]{3,2,1,0:T(8,128)}, f32[17,1,32,128]{3,2,1,0:T(8,128)}...) custom-call(f32[1,4]{1,0:T(1,128)} %add_convert_fusion.refs_0_, ...), custom_call_target="tpu_custom_call", output_to_operand_aliasing={{0}: (10, {})} | custom-call | flops 9437184000 | tf_op jit(solution)/shard_map/pointwise/pallas_call | solution.py:241
  71.8 5.8 time.5
  77.7 5.3 all-to-all-start
  83.0 19.8 %pointwise.7 = (f32[4,16,8,128,128]{4,3,2,1,0:T(8,128)}, f32[16,128,128]{2,1,0:T(8,128)}, f32[17,2,32,128]{3,2,1,0:T(8,128)}, f32[17,2,32,128]{3,2,1,0:T(8,128)}...) custom-call(f32[1,4]{1,0:T(1,128)} %add_convert_fusion.refs_0_, ...), custom_call_target="tpu_custom_call", output_to_operand_aliasing={{0}: (10, {})} | custom-call | flops 9437184000 | tf_op jit(solution)/shard_map/pointwise/pallas_call | solution.py:241
  102.8 29.2 %all-to-all-done.refs_1_ = f32[8,8,2,32,128]{4,3,2,1,0:T(8,128)S(1)} async-done(((f32[8,8,2,32,128]{4,3,2,1,0:T(8,128)}), f32[8,8,2,32,128]{4,3,2,1,0:T(8,128)S(1)}, u32[]{:S(2)}, u32[]{:S(2)}) %all-to-all-start) | async-done | bytes 2097184 | tf_op jit(solution)/shard_map/all_to_all | solution.py:445
  137.2 6.2 %collective-permute-done.6.refs_2_ = f32[17,1,32,128]{3,2,1,0:T(8,128)S(1)} collective-permute-done((f32[17,1,32,128]{3,2,1,0:T(8,128)}, f32[17,1,32,128]{3,2,1,0:T(8,128)S(1)}, u32[]{:S(2)}, u32[]{:S(2)}) %collective-permute-start.6) | collective-permute-done | bytes 278560 | tf_op jit(solution)/shard_map/ppermute | solution.py:440
  143.4 4.8 collective-permute-done.7.refs_3_
  162.3 19.7 %pointwise.8 = (f32[4,16,8,128,128]{4,3,2,1,0:T(8,128)}, f32[16,128,128]{2,1,0:T(8,128)}, f32[17,2,32,128]{3,2,1,0:T(8,128)}, f32[17,2,32,128]{3,2,1,0:T(8,128)}...) custom-call(f32[1,4]{1,0:T(1,128)} %add_convert_fusion.refs_0_, ...), custom_call_target="tpu_custom_call", output_to_operand_aliasing={{0}: (10, {})} | custom-call | flops 9437184000 | tf_op jit(solution)/shard_map/pointwise/pallas_call | solution.py:241
  187.2 5.9 time.7
  194.1 5.0 all-to-all-start.2
  202.7 12.7 %pointwise.9 = (f32[4,16,8,128,128]{4,3,2,1,0:T(8,128)}, f32[16,128,128]{2,1,0:T(8,128)}, f32[17,1,32,128]{3,2,1,0:T(8,128)}, f32[17,1,32,128]{3,2,1,0:T(8,128)}...) custom-call(f32[1,4]{1,0:T(1,128)} %add_convert_fusion.refs_0_, ...), custom_call_target="tpu_custom_call", output_to_operand_aliasing={{0}: (10, {})} | custom-call | flops 4718592000 | tf_op jit(solution)/shard_map/pointwise/pallas_call | solution.py:241
  218.8 7.2 %collective-permute-done.14.refs_3_ = f32[17,2,32,128]{3,2,1,0:T(8,128)S(1)} collective-permute-done((f32[17,2,32,128]{3,2,1,0:T(8,128)S(1)}, f32[17,2,32,128]{3,2,1,0:T(8,128)S(1)}, u32[]{:S(2)}, u32[]{:S(2)}) %collective-permute-start.14) | collective-permute-done | bytes 557088 | tf_op jit(solution)/shard_map/ppermute | solution.py:440
  229.0 5.9 time.8
  248.1 53.4 %all_to_all.50.refs_4_ = f32[8,8,2,32,128]{4,3,2,1,0:T(8,128)} all-to-all(f32[8,8,2,32,128]{4,3,2,1,0:T(8,128)} %time.8), channel_id=1, replica_groups=mesh['tm'=4,'space'=8] {'space'}, dimensions={0} | all-to-all | bytes 4194304 | tf_op jit(solution)/shard_map/all_to_all | solution.py:445
  306.8 25.0 %all-to-all-done.4.refs_5_ = f32[8,8,1,32,128]{4,3,2,1,0:T(8,128)S(1)} async-done(((f32[8,8,1,32,128]{4,3,2,1,0:T(8,128)}), f32[8,8,1,32,128]{4,3,2,1,0:T(8,128)S(1)}, u32[]{:S(2)}, u32[]{:S(2)}) %all-to-all-start.4) | async-done | bytes 1048608 | tf_op jit(solution)/shard_map/all_to_all | solution.py:445
  332.8 9.7 %middle.6 = f32[8,8,8,8,128]{4,3,2,1,0:T(8,128)} custom-call(f32[8,32,128]{2,1,0:T(8,128)} %multiply_add_fusion.refs_0_, f32[8,8,2,32,128]{4,3,2,1,0:T(8,128)} %copy-done.11, f32[8,8,1,32,128]{4,3,2,1,0:T(8,128)} %copy-done.16, f32[8,8,2,32,128]{4,3,2,1,0:T(8,128)} %copy-done.12, f32[8,8,2,32,128]{4,3,2,1,0:T(8,128)} %all_to_all.50.refs_4_, ...), custom_call_target="tpu_custom_call" | custom-call | flops 4718592000 | tf_op jit(solution)/shard_map/middle/pallas_call | solution.py:334
  346.1 9.6 %middle.5 = f32[8,8,8,8,128]{4,3,2,1,0:T(8,128)} custom-call(f32[8,32,128]{2,1,0:T(8,128)} %multiply_add_fusion.refs_0_, f32[8,8,2,32,128]{4,3,2,1,0:T(8,128)} %copy-done.11, f32[8,8,1,32,128]{4,3,2,1,0:T(8,128)} %copy-done.16, f32[8,8,2,32,128]{4,3,2,1,0:T(8,128)} %copy-done.12, f32[8,8,2,32,128]{4,3,2,1,0:T(8,128)} %all_to_all.50.refs_4_, ...), custom_call_target="tpu_custom_call" | custom-call | flops 4718592000 | tf_op jit(solution)/shard_map/middle/pallas_call | solution.py:334
  355.7 39.4 %all-to-all-done.5.refs_1_ = f32[8,8,8,8,128]{4,3,2,1,0:T(8,128)S(1)} async-done(((f32[8,8,8,8,128]{4,3,2,1,0:T(8,128)}), f32[8,8,8,8,128]{4,3,2,1,0:T(8,128)S(1)}, u32[]{:S(2)}, u32[]{:S(2)}) %all-to-all-start.5) | async-done | bytes 2097184 | tf_op jit(solution)/shard_map/all_to_all | solution.py:445
  396.4 4.6 all-to-all-start.6
  401.0 6.6 %untime.5 = (f32[16,8,8,128]{3,2,1,0:T(8,128)}, f32[16,8,8,128]{3,2,1,0:T(8,128)}, f32[16,8,8,128]{3,2,1,0:T(8,128)}, f32[16,8,8,128]{3,2,1,0:T(8,128)}) custom-call(s32[1,2]{1,0:T(1,128)} %add_bitcast_fusion.refs_0_, f32[8,8,8,8,128]{4,3,2,1,0:T(8,128)} %copy-done.13), custom_call_target="tpu_custom_call" | custom-call | flops 2883584000 | tf_op jit(solution)/shard_map/untime/pallas_call | solution.py:369
  411.1 9.7 %middle.4 = f32[8,8,8,8,128]{4,3,2,1,0:T(8,128)} custom-call(f32[8,32,128]{2,1,0:T(8,128)} %multiply_add_fusion.refs_0_, f32[8,8,2,32,128]{4,3,2,1,0:T(8,128)} %copy-done.11, f32[8,8,1,32,128]{4,3,2,1,0:T(8,128)} %copy-done.16, f32[8,8,2,32,128]{4,3,2,1,0:T(8,128)} %copy-done.12, f32[8,8,2,32,128]{4,3,2,1,0:T(8,128)} %all_to_all.50.refs_4_, ...), custom_call_target="tpu_custom_call" | custom-call | flops 4718592000 | tf_op jit(solution)/shard_map/middle/pallas_call | solution.py:334
  420.8 29.3 %all-to-all-done.6.refs_1_ = f32[8,8,8,8,128]{4,3,2,1,0:T(8,128)} async-done(((f32[8,8,8,8,128]{4,3,2,1,0:T(8,128)}), f32[8,8,8,8,128]{4,3,2,1,0:T(8,128)}, u32[]{:S(2)}, u32[]{:S(2)}) %all-to-all-start.6) | async-done | bytes 2097184 | tf_op jit(solution)/shard_map/all_to_all | solution.py:445
  455.6 6.6 %untime.6 = (f32[16,8,8,128]{3,2,1,0:T(8,128)}, f32[16,8,8,128]{3,2,1,0:T(8,128)}, f32[16,8,8,128]{3,2,1,0:T(8,128)}, f32[16,8,8,128]{3,2,1,0:T(8,128)}) custom-call(s32[1,2]{1,0:T(1,128)} %add_bitcast_fusion.refs_0_, f32[8,8,8,8,128]{4,3,2,1,0:T(8,128)} %all-to-all-done.6.refs_1_), custom_call_target="tpu_custom_call" | custom-call | flops 2883584000 | tf_op jit(solution)/shard_map/untime/pallas_call | solution.py:369
  465.7 9.6 %middle.7 = (f32[8,8,4,8,128]{4,3,2,1,0:T(8,128)}, f32[8,8,4,8,128]{4,3,2,1,0:T(8,128)}) custom-call(f32[8,32,128]{2,1,0:T(8,128)} %multiply_add_fusion.refs_0_, f32[8,8,2,32,128]{4,3,2,1,0:T(8,128)} %copy-done.11, f32[8,8,1,32,128]{4,3,2,1,0:T(8,128)} %copy-done.16, f32[8,8,2,32,128]{4,3,2,1,0:T(8,128)} %copy-done.12, ...), custom_call_target="tpu_custom_call" | custom-call | flops 4718592000 | tf_op jit(solution)/shard_map/middle/pallas_call | solution.py:334
  475.3 29.4 %all-to-all-done.7.refs_1_ = f32[8,8,8,8,128]{4,3,2,1,0:T(8,128)} async-done(((f32[8,8,8,8,128]{4,3,2,1,0:T(8,128)}), f32[8,8,8,8,128]{4,3,2,1,0:T(8,128)}, u32[]{:S(2)}, u32[]{:S(2)}) %all-to-all-start.7) | async-done | bytes 2097184 | tf_op jit(solution)/shard_map/all_to_all | solution.py:445
  508.3 6.7 %untime.7 = (f32[16,8,8,128]{3,2,1,0:T(8,128)}, f32[16,8,8,128]{3,2,1,0:T(8,128)}, f32[16,8,8,128]{3,2,1,0:T(8,128)}, f32[16,8,8,128]{3,2,1,0:T(8,128)}) custom-call(s32[1,2]{1,0:T(1,128)} %add_bitcast_fusion.refs_0_, f32[8,8,8,8,128]{4,3,2,1,0:T(8,128)} %all-to-all-done.7.refs_1_), custom_call_target="tpu_custom_call" | custom-call | flops 2883584000 | tf_op jit(solution)/shard_map/untime/pallas_call | solution.py:369
  515.0 19.8 %all-to-all-done.8.refs_1_ = f32[8,8,4,8,128]{4,3,2,1,0:T(8,128)S(1)} async-done(((f32[8,8,4,8,128]{4,3,2,1,0:T(8,128)}), f32[8,8,4,8,128]{4,3,2,1,0:T(8,128)S(1)}, u32[]{:S(2)}, u32[]{:S(2)}) %all-to-all-start.8) | async-done | bytes 1048608 | tf_op jit(solution)/shard_map/all_to_all | solution.py:445
  549.4 4.9 collective-permute-done.25.refs_9_
  557.7 9.4 %collective-permute-done.26.refs_10_ = f32[16,8,8,128]{3,2,1,0:T(8,128)S(1)} collective-permute-done((f32[16,8,8,128]{3,2,1,0:T(8,128)}, f32[16,8,8,128]{3,2,1,0:T(8,128)S(1)}, u32[]{:S(2)}, u32[]{:S(2)}) %collective-permute-start.26) | collective-permute-done | bytes 524320 | tf_op jit(solution)/shard_map/ppermute | solution.py:440
  578.4 8.0 %back.2.refs_18_ = f32[16,8,128,128]{3,2,1,0:T(8,128)} custom-call(f32[16,8,8,128]{3,2,1,0:T(8,128)} %get-tuple-element.166.refs_0_, f32[16,8,8,128]{3,2,1,0:T(8,128)} %copy-done.2, f32[16,8,8,128]{3,2,1,0:T(8,128)} %copy-done.3, f32[16,8,8,128]{3,2,1,0:T(8,128)} %copy-done.4, f32[16,8,8,128]{3,2,1,0:T(8,128)} %get-tuple-element.177.refs_4_, ...), custom_call_target="tpu_custom_call" | custom-call | flops 3670016000 | tf_op jit(solution)/shard_map/back/pallas_call | solution.py:417
  589.7 8.0 %back.3 = f32[16,8,128,128]{3,2,1,0:T(8,128)} custom-call(f32[16,8,8,128]{3,2,1,0:T(8,128)} %get-tuple-element.166.refs_0_, f32[16,8,8,128]{3,2,1,0:T(8,128)} %copy-done.2, f32[16,8,8,128]{3,2,1,0:T(8,128)} %copy-done.3, f32[16,8,8,128]{3,2,1,0:T(8,128)} %copy-done.4, f32[16,8,8,128]{3,2,1,0:T(8,128)} %get-tuple-element.177.refs_4_, ...), custom_call_target="tpu_custom_call", output_to_operand_aliasing={{}: (18, {})} | custom-call | flops 3670016000 | tf_op jit(solution)/shard_map/back/pallas_call | solution.py:417
  (189 shorter events, 133.0 us)
Async XLA Ops:
  3.9 41.4 %collective-permute-start.4 = (f32[1,5,128,128]{3,2,1,0:T(8,128)S(1)}, f32[1,5,128,128]{3,2,1,0:T(8,128)S(1)}, u32[]{:S(2)}, u32[]{:S(2)}) collective-permute-start(f32[1,5,128,128]{3,2,1,0:T(8,128)S(1)} %slice.10), channel_id=1, source_target_pairs={{8,0},{16,8},{24,16},{9,1},{17,9},{25,17},{10,2},{18,10},{26,18},{... | collective-permute-start | bytes 983048 | tf_op jit(solution)/shard_map/ppermute | solution.py:434
  6.5 38.8 %collective-permute-start.5 = (f32[16,1,128,128]{3,2,1,0:T(8,128)S(1)}, f32[16,1,128,128]{3,2,1,0:T(8,128)S(1)}, u32[]{:S(2)}, u32[]{:S(2)}) collective-permute-start(f32[16,1,128,128]{3,2,1,0:T(8,128)S(1)} %slice.11), channel_id=1, source_target_pairs={{1,0},{2,1},{3,2},{4,3},{5,4},{6,5},{7,6},{9,8},{10,9},{11,10},{12... | collective-permute-start | bytes 3145736 | tf_op jit(solution)/shard_map/ppermute | solution.py:434
  39.2 27.4 %collective-permute-start.1 = (f32[17,2,32,128]{3,2,1,0:T(8,128)}, f32[17,2,32,128]{3,2,1,0:T(8,128)S(1)}, u32[]{:S(2)}, u32[]{:S(2)}) collective-permute-start(f32[17,2,32,128]{3,2,1,0:T(8,128)} %get-tuple-element.104), channel_id=1, source_target_pairs={{0,8},{8,0},{16,24},{24,16},{1,9},{9,1},{17,25},{25,17},{2,10},{10... | collective-permute-start | bytes 1671176 | tf_op jit(solution)/shard_map/ppermute | solution.py:440
  42.2 28.6 %collective-permute-start.2 = (f32[17,2,32,128]{3,2,1,0:T(8,128)}, f32[17,2,32,128]{3,2,1,0:T(8,128)S(1)}, u32[]{:S(2)}, u32[]{:S(2)}) collective-permute-start(f32[17,2,32,128]{3,2,1,0:T(8,128)} %get-tuple-element.105), channel_id=1, source_target_pairs={{0,16},{8,24},{16,0},{24,8},{1,17},{9,25},{17,1},{25,9},{2,18},{10... | collective-permute-start | bytes 1671176 | tf_op jit(solution)/shard_map/ppermute | solution.py:440
  45.3 25.5 %collective-permute-start.3 = (f32[17,2,32,128]{3,2,1,0:T(8,128)}, f32[17,2,32,128]{3,2,1,0:T(8,128)S(1)}, u32[]{:S(2)}, u32[]{:S(2)}) collective-permute-start(f32[17,2,32,128]{3,2,1,0:T(8,128)} %get-tuple-element.106), channel_id=1, source_target_pairs={{0,24},{8,16},{16,8},{24,0},{1,25},{9,17},{17,9},{25,1},{2,26},{10... | collective-permute-start | bytes 1671176 | tf_op jit(solution)/shard_map/ppermute | solution.py:440
  77.7 54.3 %all-to-all-start = ((f32[8,8,2,32,128]{4,3,2,1,0:T(8,128)}), f32[8,8,2,32,128]{4,3,2,1,0:T(8,128)S(1)}, u32[]{:S(2)}, u32[]{:S(2)}) async-start(f32[8,8,2,32,128]{4,3,2,1,0:T(8,128)} %time.5), calls=%async_computation | async-start | bytes 4194304 | tf_op jit(solution)/shard_map/all_to_all | solution.py:445
  132.0 22.5 %collective-permute-start.9 = (f32[16,128,128]{2,1,0:T(8,128)}, f32[16,128,128]{2,1,0:T(8,128)S(1)}, u32[]{:S(2)}, u32[]{:S(2)}) collective-permute-start(f32[16,128,128]{2,1,0:T(8,128)} %get-tuple-element.127), channel_id=1, source_target_pairs={{0,1},{1,2},{2,3},{3,4},{4,5},{5,6},{6,7},{8,9},{9,10},{10,11},{11... | collective-permute-start | bytes 3145736 | tf_op jit(solution)/shard_map/ppermute | solution.py:434
  154.6 38.5 %all-to-all-start.1 = ((f32[8,8,1,32,128]{4,3,2,1,0:T(8,128)}), f32[8,8,1,32,128]{4,3,2,1,0:T(8,128)S(1)}, u32[]{:S(2)}, u32[]{:S(2)}) async-start(f32[8,8,1,32,128]{4,3,2,1,0:T(8,128)} %time.6), calls=%async_computation.1 | async-start | bytes 2097152 | tf_op jit(solution)/shard_map/all_to_all | solution.py:445
  158.8 23.3 %collective-permute-start.10 = (f32[17,2,32,128]{3,2,1,0:T(8,128)}, f32[17,2,32,128]{3,2,1,0:T(8,128)S(1)}, u32[]{:S(2)}, u32[]{:S(2)}) collective-permute-start(f32[17,2,32,128]{3,2,1,0:T(8,128)} %get-tuple-element.130), channel_id=1, source_target_pairs={{0,8},{8,0},{16,24},{24,16},{1,9},{9,1},{17,25},{25,17},{2,10},{10... | collective-permute-start | bytes 1671176 | tf_op jit(solution)/shard_map/ppermute | solution.py:440
  159.4 26.4 %collective-permute-start.11 = (f32[17,2,32,128]{3,2,1,0:T(8,128)}, f32[17,2,32,128]{3,2,1,0:T(8,128)S(1)}, u32[]{:S(2)}, u32[]{:S(2)}) collective-permute-start(f32[17,2,32,128]{3,2,1,0:T(8,128)} %get-tuple-element.131), channel_id=1, source_target_pairs={{0,16},{8,24},{16,0},{24,8},{1,17},{9,25},{17,1},{25,9},{2,18},{10... | collective-permute-start | bytes 1671176 | tf_op jit(solution)/shard_map/ppermute | solution.py:440
  161.3 25.1 %collective-permute-start.12 = (f32[17,2,32,128]{3,2,1,0:T(8,128)S(1)}, f32[17,2,32,128]{3,2,1,0:T(8,128)S(1)}, u32[]{:S(2)}, u32[]{:S(2)}) collective-permute-start(f32[17,2,32,128]{3,2,1,0:T(8,128)S(1)} %copy-done.28), channel_id=1, source_target_pairs={{0,24},{8,16},{16,8},{24,0},{1,25},{9,17},{17,9},{25,1},{2,26},{10... | collective-permute-start | bytes 1671176 | tf_op jit(solution)/shard_map/ppermute | solution.py:440
  194.1 54.0 %all-to-all-start.2 = ((f32[8,8,2,32,128]{4,3,2,1,0:T(8,128)}), f32[8,8,2,32,128]{4,3,2,1,0:T(8,128)S(1)}, u32[]{:S(2)}, u32[]{:S(2)}) async-start(f32[8,8,2,32,128]{4,3,2,1,0:T(8,128)} %time.7), calls=%async_computation.2 | async-start | bytes 4194304 | tf_op jit(solution)/shard_map/all_to_all | solution.py:445
  200.6 25.4 %collective-permute-start.14 = (f32[17,2,32,128]{3,2,1,0:T(8,128)S(1)}, f32[17,2,32,128]{3,2,1,0:T(8,128)S(1)}, u32[]{:S(2)}, u32[]{:S(2)}) collective-permute-start(f32[17,2,32,128]{3,2,1,0:T(8,128)S(1)} %copy-done.30), channel_id=1, source_target_pairs={{0,16},{8,24},{16,0},{24,8},{1,17},{9,25},{17,1},{25,9},{2,18},{10... | collective-permute-start | bytes 1671176 | tf_op jit(solution)/shard_map/ppermute | solution.py:440
  201.6 26.5 %collective-permute-start.15 = (f32[17,2,32,128]{3,2,1,0:T(8,128)S(1)}, f32[17,2,32,128]{3,2,1,0:T(8,128)S(1)}, u32[]{:S(2)}, u32[]{:S(2)}) collective-permute-start(f32[17,2,32,128]{3,2,1,0:T(8,128)S(1)} %copy-done.29), channel_id=1, source_target_pairs={{0,24},{8,16},{16,8},{24,0},{1,25},{9,17},{17,9},{25,1},{2,26},{10... | collective-permute-start | bytes 1671176 | tf_op jit(solution)/shard_map/ppermute | solution.py:440
  217.8 21.9 %collective-permute-start.18 = (f32[17,1,32,128]{3,2,1,0:T(8,128)}, f32[17,1,32,128]{3,2,1,0:T(8,128)S(1)}, u32[]{:S(2)}, u32[]{:S(2)}) collective-permute-start(f32[17,1,32,128]{3,2,1,0:T(8,128)} %get-tuple-element.156), channel_id=1, source_target_pairs={{0,24},{8,16},{16,8},{24,0},{1,25},{9,17},{17,9},{25,1},{2,26},{10... | collective-permute-start | bytes 835592 | tf_op jit(solution)/shard_map/ppermute | solution.py:440
  301.6 30.2 %all-to-all-start.4 = ((f32[8,8,1,32,128]{4,3,2,1,0:T(8,128)}), f32[8,8,1,32,128]{4,3,2,1,0:T(8,128)S(1)}, u32[]{:S(2)}, u32[]{:S(2)}) async-start(f32[8,8,1,32,128]{4,3,2,1,0:T(8,128)} %time.9), calls=%async_computation.4 | async-start | bytes 2097152 | tf_op jit(solution)/shard_map/all_to_all | solution.py:445
  342.4 52.6 %all-to-all-start.5 = ((f32[8,8,8,8,128]{4,3,2,1,0:T(8,128)}), f32[8,8,8,8,128]{4,3,2,1,0:T(8,128)S(1)}, u32[]{:S(2)}, u32[]{:S(2)}) async-start(f32[8,8,8,8,128]{4,3,2,1,0:T(8,128)} %middle.6), calls=%async_computation.5 | async-start | bytes 4194304 | tf_op jit(solution)/shard_map/all_to_all | solution.py:445
  396.4 53.6 %all-to-all-start.6 = ((f32[8,8,8,8,128]{4,3,2,1,0:T(8,128)}), f32[8,8,8,8,128]{4,3,2,1,0:T(8,128)}, u32[]{:S(2)}, u32[]{:S(2)}) async-start(f32[8,8,8,8,128]{4,3,2,1,0:T(8,128)} %middle.5), calls=%async_computation.6 | async-start | bytes 4194304 | tf_op jit(solution)/shard_map/all_to_all | solution.py:445
  407.6 42.4 %collective-permute-start.19 = (f32[16,8,8,128]{3,2,1,0:T(8,128)}, f32[16,8,8,128]{3,2,1,0:T(8,128)S(1)}, u32[]{:S(2)}, u32[]{:S(2)}) collective-permute-start(f32[16,8,8,128]{3,2,1,0:T(8,128)} %get-tuple-element.163), channel_id=1, source_target_pairs={{0,8},{8,0},{16,24},{24,16},{1,9},{9,1},{17,25},{25,17},{2,10},{10... | collective-permute-start | bytes 1572872 | tf_op jit(solution)/shard_map/ppermute | solution.py:440
  409.1 41.0 %collective-permute-start.20 = (f32[16,8,8,128]{3,2,1,0:T(8,128)}, f32[16,8,8,128]{3,2,1,0:T(8,128)S(1)}, u32[]{:S(2)}, u32[]{:S(2)}) collective-permute-start(f32[16,8,8,128]{3,2,1,0:T(8,128)} %get-tuple-element.164), channel_id=1, source_target_pairs={{0,16},{8,24},{16,0},{24,8},{1,17},{9,25},{17,1},{25,9},{2,18},{10... | collective-permute-start | bytes 1572872 | tf_op jit(solution)/shard_map/ppermute | solution.py:440
  410.1 40.0 %collective-permute-start.21 = (f32[16,8,8,128]{3,2,1,0:T(8,128)}, f32[16,8,8,128]{3,2,1,0:T(8,128)S(1)}, u32[]{:S(2)}, u32[]{:S(2)}) collective-permute-start(f32[16,8,8,128]{3,2,1,0:T(8,128)} %get-tuple-element.165), channel_id=1, source_target_pairs={{0,24},{8,16},{16,8},{24,0},{1,25},{9,17},{17,9},{25,1},{2,26},{10... | collective-permute-start | bytes 1572872 | tf_op jit(solution)/shard_map/ppermute | solution.py:440
  451.3 53.4 %all-to-all-start.7 = ((f32[8,8,8,8,128]{4,3,2,1,0:T(8,128)}), f32[8,8,8,8,128]{4,3,2,1,0:T(8,128)}, u32[]{:S(2)}, u32[]{:S(2)}) async-start(f32[8,8,8,8,128]{4,3,2,1,0:T(8,128)} %middle.4), calls=%async_computation.7 | async-start | bytes 4194304 | tf_op jit(solution)/shard_map/all_to_all | solution.py:445
  462.2 42.5 %collective-permute-start.22 = (f32[16,8,8,128]{3,2,1,0:T(8,128)}, f32[16,8,8,128]{3,2,1,0:T(8,128)S(1)}, u32[]{:S(2)}, u32[]{:S(2)}) collective-permute-start(f32[16,8,8,128]{3,2,1,0:T(8,128)} %get-tuple-element.174), channel_id=1, source_target_pairs={{0,8},{8,0},{16,24},{24,16},{1,9},{9,1},{17,25},{25,17},{2,10},{10... | collective-permute-start | bytes 1572872 | tf_op jit(solution)/shard_map/ppermute | solution.py:440
  463.7 41.0 %collective-permute-start.23 = (f32[16,8,8,128]{3,2,1,0:T(8,128)}, f32[16,8,8,128]{3,2,1,0:T(8,128)S(1)}, u32[]{:S(2)}, u32[]{:S(2)}) collective-permute-start(f32[16,8,8,128]{3,2,1,0:T(8,128)} %get-tuple-element.175), channel_id=1, source_target_pairs={{0,16},{8,24},{16,0},{24,8},{1,17},{9,25},{17,1},{25,9},{2,18},{10... | collective-permute-start | bytes 1572872 | tf_op jit(solution)/shard_map/ppermute | solution.py:440
  464.7 40.0 %collective-permute-start.24 = (f32[16,8,8,128]{3,2,1,0:T(8,128)}, f32[16,8,8,128]{3,2,1,0:T(8,128)S(1)}, u32[]{:S(2)}, u32[]{:S(2)}) collective-permute-start(f32[16,8,8,128]{3,2,1,0:T(8,128)} %get-tuple-element.176), channel_id=1, source_target_pairs={{0,24},{8,16},{16,8},{24,0},{1,25},{9,17},{17,9},{25,1},{2,26},{10... | collective-permute-start | bytes 1572872 | tf_op jit(solution)/shard_map/ppermute | solution.py:440
  504.7 30.1 %all-to-all-start.8 = ((f32[8,8,4,8,128]{4,3,2,1,0:T(8,128)}), f32[8,8,4,8,128]{4,3,2,1,0:T(8,128)S(1)}, u32[]{:S(2)}, u32[]{:S(2)}) async-start(f32[8,8,4,8,128]{4,3,2,1,0:T(8,128)} %get-tuple-element.182), calls=%async_computation.8 | async-start | bytes 2097152 | tf_op jit(solution)/shard_map/all_to_all | solution.py:445
  535.8 31.3 %all-to-all-start.9 = ((f32[8,8,4,8,128]{4,3,2,1,0:T(8,128)}), f32[8,8,4,8,128]{4,3,2,1,0:T(8,128)S(1)}, u32[]{:S(2)}, u32[]{:S(2)}) async-start(f32[8,8,4,8,128]{4,3,2,1,0:T(8,128)} %get-tuple-element.188), calls=%async_computation.9 | async-start | bytes 2097152 | tf_op jit(solution)/shard_map/all_to_all | solution.py:445
  540.9 26.2 %collective-permute-start.26 = (f32[16,8,8,128]{3,2,1,0:T(8,128)}, f32[16,8,8,128]{3,2,1,0:T(8,128)S(1)}, u32[]{:S(2)}, u32[]{:S(2)}) collective-permute-start(f32[16,8,8,128]{3,2,1,0:T(8,128)} %get-tuple-element.186), channel_id=1, source_target_pairs={{0,16},{8,24},{16,0},{24,8},{1,17},{9,25},{17,1},{25,9},{2,18},{10... | collective-permute-start | bytes 1572872 | tf_op jit(solution)/shard_map/ppermute | solution.py:440
  541.9 25.2 %collective-permute-start.27 = (f32[16,8,8,128]{3,2,1,0:T(8,128)}, f32[16,8,8,128]{3,2,1,0:T(8,128)S(1)}, u32[]{:S(2)}, u32[]{:S(2)}) collective-permute-start(f32[16,8,8,128]{3,2,1,0:T(8,128)} %get-tuple-element.187), channel_id=1, source_target_pairs={{0,24},{8,16},{16,8},{24,0},{1,25},{9,17},{17,9},{25,1},{2,26},{10... | collective-permute-start | bytes 1572872 | tf_op jit(solution)/shard_map/ppermute | solution.py:440
  547.0 27.8 %collective-permute-start.31 = (f32[16,4,8,128]{3,2,1,0:T(8,128)}, f32[16,4,8,128]{3,2,1,0:T(8,128)S(1)}, u32[]{:S(2)}, u32[]{:S(2)}) collective-permute-start(f32[16,4,8,128]{3,2,1,0:T(8,128)} %get-tuple-element.199), channel_id=1, source_target_pairs={{0,8},{8,0},{16,24},{24,16},{1,9},{9,1},{17,25},{25,17},{2,10},{10... | collective-permute-start | bytes 786440 | tf_op jit(solution)/shard_map/ppermute | solution.py:440
  548.4 28.0 %collective-permute-start.32 = (f32[16,4,8,128]{3,2,1,0:T(8,128)}, f32[16,4,8,128]{3,2,1,0:T(8,128)S(1)}, u32[]{:S(2)}, u32[]{:S(2)}) collective-permute-start(f32[16,4,8,128]{3,2,1,0:T(8,128)} %get-tuple-element.200), channel_id=1, source_target_pairs={{0,16},{8,24},{16,0},{24,8},{1,17},{9,25},{17,1},{25,9},{2,18},{10... | collective-permute-start | bytes 786440 | tf_op jit(solution)/shard_map/ppermute | solution.py:440
  554.4 24.1 %collective-permute-start.33 = (f32[16,4,8,128]{3,2,1,0:T(8,128)}, f32[16,4,8,128]{3,2,1,0:T(8,128)}, u32[]{:S(2)}, u32[]{:S(2)}) collective-permute-start(f32[16,4,8,128]{3,2,1,0:T(8,128)} %get-tuple-element.201), channel_id=1, source_target_pairs={{0,24},{8,16},{16,8},{24,0},{1,25},{9,17},{17,9},{25,1},{2,26},{10... | collective-permute-start | bytes 786440 | tf_op jit(solution)/shard_map/ppermute | solution.py:440
  (59 other events, 524.7 us)
